TPU v7x, 512 devices: a whole 4x8x8 slice. The times are simulated.
512 devices in a mesh: band: 32 (over z, y_hi), domain: 16 (over x, y_lo, core).
Axes of the slice: x: 4, y: 8 (y_hi: 4, y_lo: 2; y = y_hi * 2 + y_lo), z: 8, core: 2. Of those that a mesh axis runs over, the one named last changes fastest.
Arguments:
- orbitals: float32 [64, 16, 16, 16, 128], P('band', 'domain'), may hold values from -24 to 24
- potential: float32 [16, 16, 16, 128], P('domain'), may hold values from 0 to 1.5
Outputs:
- filtered: float32 [64, 16, 16, 16, 128], P('band', 'domain')
- intersection: float32 [64, 64], P('band')
- projected: float32 [64, 64], P('band')
All inputs are finite; a program needn't handle non-finite values.
Results may differ from a plain program's by a relative error of at most 0.00005.
Values sent between devices are 32-bit elements; how exact they have to be, the bound alone decides.
A program may use at most 128 MiB of HBM per device.

v0:
```python
import jax
import jax.numpy as jnp
from jax import lax
from jax.sharding import PartitionSpec as P

second_coeffs = (
    -5369.0 / 1800.0,
    12.0 / 7.0,
    -15.0 / 56.0,
    10.0 / 189.0,
    -1.0 / 112.0,
    2.0 / 1925.0,
    -1.0 / 16632.0,
)
filter_center = 6.5
filter_half = 5.5
stencil_reach = 6


def from_behind(value, axis, steps):
    count = lax.axis_size(axis)
    pairs = [(source, (source + steps) % count) for source in range(count)]
    return lax.ppermute(value, axis, pairs)


def partner(x, axis, apart):
    return lax.ppermute(x, axis, [(i, i ^ 1 << apart) for i in range(lax.axis_size(axis))])


def second_along(padded, axis, count):
    base = lax.slice_in_dim(padded, stencil_reach, stencil_reach + count, axis=axis)
    total = second_coeffs[0] * base
    for step in range(1, 7):
        ahead = lax.slice_in_dim(
            padded, stencil_reach + step, stencil_reach + step + count, axis=axis
        )
        behind = lax.slice_in_dim(
            padded, stencil_reach - step, stencil_reach - step + count, axis=axis
        )
        total = total + second_coeffs[step] * (ahead + behind)
    return total


def hamiltonian(field, grid_pot):
    count_x = field.shape[1]
    count_y = field.shape[2]
    count_z = field.shape[3]
    lower = from_behind(field[:, count_x - 6 :], "domain", 4)
    upper = from_behind(field[:, :6], "domain", -4)
    along_x = jnp.concatenate([lower, field, upper], axis=1)
    rims_y = partner(jnp.stack([field[:, :, :6], field[:, :, count_y - 6 :]]), "domain", 1)
    along_y = jnp.concatenate([rims_y[1], field, rims_y[0]], axis=2)
    rims_z = partner(jnp.stack([field[:, :, :, :6], field[:, :, :, count_z - 6 :]]), "domain", 0)
    along_z = jnp.concatenate([rims_z[1], field, rims_z[0]], axis=3)
    lap = (
        second_along(along_x, 1, count_x)
        + second_along(along_y, 2, count_y)
        + second_along(along_z, 3, count_z)
    )
    return -0.5 * lap + grid_pot * field


def contract(left, right):
    return lax.dot_general(
        left,
        right,
        (((1,), (1,)), ((), ())),
        precision=lax.Precision.HIGHEST,
        preferred_element_type=jnp.float32,
    )


def shards(orbitals, potential):
    start = orbitals[:, 0]
    grid_pot = potential[0]
    first = (hamiltonian(start, grid_pot) - filter_center * start) / filter_half
    second = 2.0 * (hamiltonian(first, grid_pot) - filter_center * first) / filter_half - start
    applied = hamiltonian(second, grid_pot)
    bands_here = start.shape[0]
    flat = second.reshape(bands_here, -1)
    hflat = applied.reshape(bands_here, -1)
    piece = lax.all_gather(flat, "band", axis=0, tiled=True)
    over_rows = contract(flat, piece)
    proj_rows = contract(hflat, piece)
    over_rows, proj_rows = (over_rows, proj_rows)
    over_sum, proj_sum = lax.psum((over_rows, proj_rows), "domain")
    cell_total = float(flat.shape[1] * lax.axis_size("domain"))
    return (second[:, None], over_sum / cell_total, proj_sum / cell_total)


def solution(mesh):
    return jax.shard_map(
        shards,
        mesh=mesh,
        in_specs=(P("band", "domain", None, None, None), P("domain", None, None, None)),
        out_specs=(P("band", "domain", None, None, None), P("band", None), P("band", None)),
        check_vma=False,
    )
```

profile of v0, /device:TPU:1, one launch (start us, length us, event | category | flops | bytes accessed | tf_op | source)
XLA Modules:
  0.0 260.3 jit_solution(17465876167294726069)
XLA Ops:
  7.2 0.0 all-gather.3.cloned.1.call-start
  7.2 1.2 slice_bitcast_fusion.5
  8.4 0.3 copy.83
  8.7 0.3 copy.82
  9.0 8.8 %collective-permute-start.3 = (f32[2,2,16,16,6]{3,2,4,1,0:T(8,128)S(1)}, f32[2,2,16,16,6]{3,2,4,1,0:T(8,128)S(1)}, u32[]{:S(2)}, u32[]{:S(2)}) collective-permute-start(f32[2,2,16,16,6]{3,2,4,1,0:T(8,128)S(1)} %pad_maximum_fusion.19), channel_id=1, source_target_pairs={{0,1},{1,0},{2,3},{3,2},{4,5},{5,4},{6,7},{7,6},{8,9},{9,8},{10,11... | collective-permute-start | bytes 73736 | tf_op jit(solution)/shard_map/ppermute | solution.py:27
  17.8 1.0 slice_bitcast_fusion.11
  18.9 1.9 collective-permute-start.2
  20.8 1.0 fusion.277
  21.8 1.9 collective-permute-start.1
  23.7 4.6 %collective-permute-start = (f32[2,6,16,128]{3,2,1,0:T(8,128)S(1)}, f32[2,6,16,128]{3,2,1,0:T(8,128)S(1)}, u32[]{:S(2)}, u32[]{:S(2)}) collective-permute-start(f32[2,6,16,128]{3,2,1,0:T(8,128)S(1)} %get-tuple-element.31), channel_id=1, source_target_pairs={{0,12},{1,13},{2,14},{3,15},{4,0},{5,1},{6,2},{7,3},{8,4},{9,5},{1... | collective-permute-start | bytes 294920 | tf_op jit(solution)/shard_map/ppermute | solution.py:23
  28.3 0.9 broadcast_multiply_fusion.1
  29.3 0.3 copy.85
  29.5 0.3 copy.84
  29.8 0.1 copy_bitcast_fusion.4
  29.9 0.3 collective-permute-done
  30.2 7.7 %broadcast_multiply_fusion = (f32[2,16,16,128]{3,2,1,0:T(8,128)S(1)}, f32[2,16,16,128]{3,2,1,0:T(8,128)S(1)}) fusion(f32[2,16,16,128]{3,2,1,0:T(8,128)} %bitcast.78, f32[16,16,128]{2,1,0:T(8,128)} %bitcast.79, f32[2,16,16,6]{3,2,1,0:T(8,128)S(1)} %copy.85, f32[2,16,16,6]{3,2,1,0:T(8,128)S(1)} %copy.84, f32[2,16,6,128]{3,2,1,0:T(8,128)S(1)} %get-tuple-element.49, ...), kind=kLoop, calls=%fused_computation.496 | loop fusion | flops 6488064 | bytes 1335296 | tf_op jit(solution)/shard_map/div | solution.py:76
  37.9 0.1 slice_bitcast_fusion.3
  38.1 1.9 collective-permute-start.5
  40.0 5.3 %collective-permute-start.4 = (f32[2,6,16,128]{3,2,1,0:T(8,128)S(1)}, f32[2,6,16,128]{3,2,1,0:T(8,128)S(1)}, u32[]{:S(2)}, u32[]{:S(2)}) collective-permute-start(f32[2,6,16,128]{3,2,1,0:T(8,128)S(1)} %get-tuple-element.29), channel_id=1, source_target_pairs={{0,12},{1,13},{2,14},{3,15},{4,0},{5,1},{6,2},{7,3},{8,4},{9,5},{1... | collective-permute-start | bytes 294920 | tf_op jit(solution)/shard_map/ppermute | solution.py:23
  45.4 0.3 copy.91
  45.6 0.3 copy.90
  46.0 3.3 %collective-permute-start.7 = (f32[2,2,16,16,6]{3,2,4,1,0:T(8,128)S(1)}, f32[2,2,16,16,6]{3,2,4,1,0:T(8,128)S(1)}, u32[]{:S(2)}, u32[]{:S(2)}) collective-permute-start(f32[2,2,16,16,6]{3,2,4,1,0:T(8,128)S(1)} %pad_maximum_fusion.21), channel_id=1, source_target_pairs={{0,1},{1,0},{2,3},{3,2},{4,5},{5,4},{6,7},{7,6},{8,9},{9,8},{10,11... | collective-permute-start | bytes 73736 | tf_op jit(solution)/shard_map/ppermute | solution.py:27
  49.3 3.4 %collective-permute-start.6 = (f32[2,2,16,6,128]{4,2,3,1,0:T(8,128)S(1)}, f32[2,2,16,6,128]{4,2,3,1,0:T(8,128)S(1)}, u32[]{:S(2)}, u32[]{:S(2)}) collective-permute-start(f32[2,2,16,6,128]{4,2,3,1,0:T(8,128)S(1)} %pad_maximum_fusion.20), channel_id=1, source_target_pairs={{0,2},{1,3},{2,0},{3,1},{4,6},{5,7},{6,4},{7,5},{8,10},{9,11},{10,... | collective-permute-start | bytes 589832 | tf_op jit(solution)/shard_map/ppermute | solution.py:27
  52.7 0.3 copy.93
  53.0 0.3 copy.92
  53.2 4.5 %collective-permute-done.6 = f32[2,2,16,6,128]{4,2,3,1,0:T(8,128)S(1)} collective-permute-done((f32[2,2,16,6,128]{4,2,3,1,0:T(8,128)S(1)}, f32[2,2,16,6,128]{4,2,3,1,0:T(8,128)S(1)}, u32[]{:S(2)}, u32[]{:S(2)}) %collective-permute-start.6) | collective-permute-done | bytes 196640 | tf_op jit(solution)/shard_map/ppermute | solution.py:27
  57.9 1.8 fusion.41
  59.7 0.0 copy-start.1
  59.7 0.9 reshape.14
  60.6 0.0 all-gather.3.cloned.1.call-update
  60.6 1.9 collective-permute-start.9
  62.5 4.6 %collective-permute-start.8 = (f32[2,6,16,128]{3,2,1,0:T(8,128)S(1)}, f32[2,6,16,128]{3,2,1,0:T(8,128)S(1)}, u32[]{:S(2)}, u32[]{:S(2)}) collective-permute-start(f32[2,6,16,128]{3,2,1,0:T(8,128)S(1)} %get-tuple-element.23), channel_id=1, source_target_pairs={{0,12},{1,13},{2,14},{3,15},{4,0},{5,1},{6,2},{7,3},{8,4},{9,5},{1... | collective-permute-start | bytes 294920 | tf_op jit(solution)/shard_map/ppermute | solution.py:23
  67.2 0.1 slice_bitcast_fusion.1
  67.3 0.3 copy.99
  67.6 0.3 copy.98
  67.9 3.3 %collective-permute-start.11 = (f32[2,2,16,16,6]{3,2,4,1,0:T(8,128)S(1)}, f32[2,2,16,16,6]{3,2,4,1,0:T(8,128)S(1)}, u32[]{:S(2)}, u32[]{:S(2)}) collective-permute-start(f32[2,2,16,16,6]{3,2,4,1,0:T(8,128)S(1)} %pad_maximum_fusion.23), channel_id=1, source_target_pairs={{0,1},{1,0},{2,3},{3,2},{4,5},{5,4},{6,7},{7,6},{8,9},{9,8},{10,11... | collective-permute-start | bytes 73736 | tf_op jit(solution)/shard_map/ppermute | solution.py:27
  71.2 3.5 %collective-permute-start.10 = (f32[2,2,16,6,128]{4,2,3,1,0:T(8,128)S(1)}, f32[2,2,16,6,128]{4,2,3,1,0:T(8,128)S(1)}, u32[]{:S(2)}, u32[]{:S(2)}) collective-permute-start(f32[2,2,16,6,128]{4,2,3,1,0:T(8,128)S(1)} %pad_maximum_fusion.22), channel_id=1, source_target_pairs={{0,2},{1,3},{2,0},{3,1},{4,6},{5,7},{6,4},{7,5},{8,10},{9,11},{10,... | collective-permute-start | bytes 589832 | tf_op jit(solution)/shard_map/ppermute | solution.py:27
  74.8 0.3 copy.101
  75.1 0.3 copy.100
  75.4 7.4 %collective-permute-done.10 = f32[2,2,16,6,128]{4,2,3,1,0:T(8,128)S(1)} collective-permute-done((f32[2,2,16,6,128]{4,2,3,1,0:T(8,128)S(1)}, f32[2,2,16,6,128]{4,2,3,1,0:T(8,128)S(1)}, u32[]{:S(2)}, u32[]{:S(2)}) %collective-permute-start.10) | collective-permute-done | bytes 196640 | tf_op jit(solution)/shard_map/ppermute | solution.py:27
  82.8 1.8 fusion.8
  84.6 113.5 %all-gather.3.cloned.1.call-done = f32[32,2,32768]{2,1,0:T(2,128)} async-done(((f32[1,2,32768]{2,1,0:T(2,128)}), f32[32,2,32768]{2,1,0:T(2,128)}) %all-gather.3.cloned.1.call-update) | async-done | bytes 8388624 | tf_op jit(solution)/shard_map/all_gather | solution.py:82
  198.1 10.9 %reshape.15 = f32[64,32768]{1,0:T(8,128)} reshape(f32[32,2,32768]{2,1,0:T(2,128)} %all-gather.3.cloned.1.call-done) | data formatting | bytes 16777216
  209.0 9.1 %fusion.253 = f32[2,64]{1,0:T(2,128)S(1)} fusion(f32[64,32768]{1,0:T(8,128)} %reshape.15, f32[1,2,256,128]{3,2,1,0:T(8,128)S(1)} %bitcast.73), kind=kOutput, calls=%fused_computation.433 | convolution fusion | flops 50331648 | bytes 8651264 | tf_op jit(solution)/shard_map/dot_general | solution.py:64
  218.1 6.6 %fusion.250 = f32[2,64]{1,0:T(2,128)S(1)} fusion(f32[64,32768]{1,0:T(8,128)S(1)} %copy-done, f32[1,2,256,128]{3,2,1,0:T(8,128)S(1)} %bitcast.81), kind=kOutput, calls=%fused_computation.430 | convolution fusion | flops 50331648 | bytes 8651264 | tf_op jit(solution)/shard_map/dot_general | solution.py:64
  224.7 27.6 %all-reduce = (f32[2,64]{1,0:T(2,128)S(1)}, f32[2,64]{1,0:T(2,128)S(1)}) all-reduce(f32[2,64]{1,0:T(2,128)S(1)} %fusion.253, f32[2,64]{1,0:T(2,128)S(1)} %fusion.250), channel_id=1, replica_groups=mesh['band'=32,'domain'=16] {'domain'}, use_global_device_ids=true, to_apply=%region_0.0 | all-reduce | flops 256 | bytes 2048 | tf_op jit(solution)/shard_map/psum | solution.py:86
  252.3 0.6 broadcast_multiply_fusion.3
  252.8 0.6 broadcast_multiply_fusion.2
  (42 shorter events, 0.6 us)
Async XLA Ops:
  7.2 50.7 %copy-start.2 = (f32[2,1,16,16,128]{4,3,2,1,0:T(8,128)S(1)}, f32[2,1,16,16,128]{4,3,2,1,0:T(8,128)}, u32[]{:S(2)}) copy-start(f32[2,1,16,16,128]{4,3,2,1,0:T(8,128)} %param.2) | copy-start | bytes 786436
  7.2 191.0 %all-gather.3.cloned.1.call-start = ((), (), s32[]{:S(2)}) async-start(), calls=%async_computation | async-start | bytes 8650752 | tf_op jit(solution)/shard_map/all_gather | solution.py:82
  9.0 20.2 %collective-permute-start.3 = (f32[2,2,16,16,6]{3,2,4,1,0:T(8,128)S(1)}, f32[2,2,16,16,6]{3,2,4,1,0:T(8,128)S(1)}, u32[]{:S(2)}, u32[]{:S(2)}) collective-permute-start(f32[2,2,16,16,6]{3,2,4,1,0:T(8,128)S(1)} %pad_maximum_fusion.19), channel_id=1, source_target_pairs={{0,1},{1,0},{2,3},{3,2},{4,5},{5,4},{6,7},{7,6},{8,9},{9,8},{10,11... | collective-permute-start | bytes 73736 | tf_op jit(solution)/shard_map/ppermute | solution.py:27
  18.9 10.9 %collective-permute-start.2 = (f32[2,2,16,6,128]{4,2,3,1,0:T(8,128)S(1)}, f32[2,2,16,6,128]{4,2,3,1,0:T(8,128)S(1)}, u32[]{:S(2)}, u32[]{:S(2)}) collective-permute-start(f32[2,2,16,6,128]{4,2,3,1,0:T(8,128)S(1)} %pad_maximum_fusion.18), channel_id=1, source_target_pairs={{0,2},{1,3},{2,0},{3,1},{4,6},{5,7},{6,4},{7,5},{8,10},{9,11},{10,... | collective-permute-start | bytes 589832 | tf_op jit(solution)/shard_map/ppermute | solution.py:27
  21.8 8.1 %collective-permute-start.1 = (f32[2,6,16,128]{3,2,1,0:T(8,128)S(1)}, f32[2,6,16,128]{3,2,1,0:T(8,128)S(1)}, u32[]{:S(2)}, u32[]{:S(2)}) collective-permute-start(f32[2,6,16,128]{3,2,1,0:T(8,128)S(1)} %get-tuple-element.32), channel_id=1, source_target_pairs={{0,4},{1,5},{2,6},{3,7},{4,8},{5,9},{6,10},{7,11},{8,12},{9,13},{1... | collective-permute-start | bytes 294920 | tf_op jit(solution)/shard_map/ppermute | solution.py:23
  23.7 6.5 %collective-permute-start = (f32[2,6,16,128]{3,2,1,0:T(8,128)S(1)}, f32[2,6,16,128]{3,2,1,0:T(8,128)S(1)}, u32[]{:S(2)}, u32[]{:S(2)}) collective-permute-start(f32[2,6,16,128]{3,2,1,0:T(8,128)S(1)} %get-tuple-element.31), channel_id=1, source_target_pairs={{0,12},{1,13},{2,14},{3,15},{4,0},{5,1},{6,2},{7,3},{8,4},{9,5},{1... | collective-permute-start | bytes 294920 | tf_op jit(solution)/shard_map/ppermute | solution.py:23
  29.9 52.9 %copy-start.3 = (f32[1,16,16,128]{3,2,1,0:T(8,128)S(1)}, f32[1,16,16,128]{3,2,1,0:T(8,128)}, u32[]{:S(2)}) copy-start(f32[1,16,16,128]{3,2,1,0:T(8,128)} %param.3) | copy-start | bytes 393220
  38.1 19.8 %collective-permute-start.5 = (f32[2,6,16,128]{3,2,1,0:T(8,128)S(1)}, f32[2,6,16,128]{3,2,1,0:T(8,128)S(1)}, u32[]{:S(2)}, u32[]{:S(2)}) collective-permute-start(f32[2,6,16,128]{3,2,1,0:T(8,128)S(1)} %get-tuple-element.30), channel_id=1, source_target_pairs={{0,4},{1,5},{2,6},{3,7},{4,8},{5,9},{6,10},{7,11},{8,12},{9,13},{1... | collective-permute-start | bytes 294920 | tf_op jit(solution)/shard_map/ppermute | solution.py:23
  40.0 17.9 %collective-permute-start.4 = (f32[2,6,16,128]{3,2,1,0:T(8,128)S(1)}, f32[2,6,16,128]{3,2,1,0:T(8,128)S(1)}, u32[]{:S(2)}, u32[]{:S(2)}) collective-permute-start(f32[2,6,16,128]{3,2,1,0:T(8,128)S(1)} %get-tuple-element.29), channel_id=1, source_target_pairs={{0,12},{1,13},{2,14},{3,15},{4,0},{5,1},{6,2},{7,3},{8,4},{9,5},{1... | collective-permute-start | bytes 294920 | tf_op jit(solution)/shard_map/ppermute | solution.py:23
  46.0 6.7 %collective-permute-start.7 = (f32[2,2,16,16,6]{3,2,4,1,0:T(8,128)S(1)}, f32[2,2,16,16,6]{3,2,4,1,0:T(8,128)S(1)}, u32[]{:S(2)}, u32[]{:S(2)}) collective-permute-start(f32[2,2,16,16,6]{3,2,4,1,0:T(8,128)S(1)} %pad_maximum_fusion.21), channel_id=1, source_target_pairs={{0,1},{1,0},{2,3},{3,2},{4,5},{5,4},{6,7},{7,6},{8,9},{9,8},{10,11... | collective-permute-start | bytes 73736 | tf_op jit(solution)/shard_map/ppermute | solution.py:27
  49.3 8.4 %collective-permute-start.6 = (f32[2,2,16,6,128]{4,2,3,1,0:T(8,128)S(1)}, f32[2,2,16,6,128]{4,2,3,1,0:T(8,128)S(1)}, u32[]{:S(2)}, u32[]{:S(2)}) collective-permute-start(f32[2,2,16,6,128]{4,2,3,1,0:T(8,128)S(1)} %pad_maximum_fusion.20), channel_id=1, source_target_pairs={{0,2},{1,3},{2,0},{3,1},{4,6},{5,7},{6,4},{7,5},{8,10},{9,11},{10,... | collective-permute-start | bytes 589832 | tf_op jit(solution)/shard_map/ppermute | solution.py:27
  59.7 149.4 %copy-start.1 = (f32[2,16,16,128]{3,2,1,0:T(8,128)}, f32[2,16,16,128]{3,2,1,0:T(8,128)S(1)}, u32[]{:S(2)}) copy-start(f32[2,16,16,128]{3,2,1,0:T(8,128)S(1)} %fusion.41) | copy-start | bytes 786436
  60.6 22.2 %collective-permute-start.9 = (f32[2,6,16,128]{3,2,1,0:T(8,128)S(1)}, f32[2,6,16,128]{3,2,1,0:T(8,128)S(1)}, u32[]{:S(2)}, u32[]{:S(2)}) collective-permute-start(f32[2,6,16,128]{3,2,1,0:T(8,128)S(1)} %get-tuple-element.24), channel_id=1, source_target_pairs={{0,4},{1,5},{2,6},{3,7},{4,8},{5,9},{6,10},{7,11},{8,12},{9,13},{1... | collective-permute-start | bytes 294920 | tf_op jit(solution)/shard_map/ppermute | solution.py:23
  62.5 20.3 %collective-permute-start.8 = (f32[2,6,16,128]{3,2,1,0:T(8,128)S(1)}, f32[2,6,16,128]{3,2,1,0:T(8,128)S(1)}, u32[]{:S(2)}, u32[]{:S(2)}) collective-permute-start(f32[2,6,16,128]{3,2,1,0:T(8,128)S(1)} %get-tuple-element.23), channel_id=1, source_target_pairs={{0,12},{1,13},{2,14},{3,15},{4,0},{5,1},{6,2},{7,3},{8,4},{9,5},{1... | collective-permute-start | bytes 294920 | tf_op jit(solution)/shard_map/ppermute | solution.py:23
  67.9 6.8 %collective-permute-start.11 = (f32[2,2,16,16,6]{3,2,4,1,0:T(8,128)S(1)}, f32[2,2,16,16,6]{3,2,4,1,0:T(8,128)S(1)}, u32[]{:S(2)}, u32[]{:S(2)}) collective-permute-start(f32[2,2,16,16,6]{3,2,4,1,0:T(8,128)S(1)} %pad_maximum_fusion.23), channel_id=1, source_target_pairs={{0,1},{1,0},{2,3},{3,2},{4,5},{5,4},{6,7},{7,6},{8,9},{9,8},{10,11... | collective-permute-start | bytes 73736 | tf_op jit(solution)/shard_map/ppermute | solution.py:27
  71.2 11.5 %collective-permute-start.10 = (f32[2,2,16,6,128]{4,2,3,1,0:T(8,128)S(1)}, f32[2,2,16,6,128]{4,2,3,1,0:T(8,128)S(1)}, u32[]{:S(2)}, u32[]{:S(2)}) collective-permute-start(f32[2,2,16,6,128]{4,2,3,1,0:T(8,128)S(1)} %pad_maximum_fusion.22), channel_id=1, source_target_pairs={{0,2},{1,3},{2,0},{3,1},{4,6},{5,7},{6,4},{7,5},{8,10},{9,11},{10,... | collective-permute-start | bytes 589832 | tf_op jit(solution)/shard_map/ppermute | solution.py:27
  209.0 9.1 %copy-start = (f32[64,32768]{1,0:T(8,128)S(1)}, f32[64,32768]{1,0:T(8,128)}, u32[]{:S(2)}) copy-start(f32[64,32768]{1,0:T(8,128)} %reshape.15) | copy-start | bytes 25165828
Sparse Core Ops, SparseCore 0:
  60.7 137.4 all-gather.2
where the time goes:
time: 263 us; the launch traced here: 260 us
  waiting for transfers between devices  126 us (48%)
  starting transfers between devices  44.4 us (17%)
  blocking collectives  27.6 us (10%)
  local copies, waits for them, and re-layouts  18.9 us (7%)
  matrix products  15.7 us (6%)
  between operations  14.5 us (6%)
  other arithmetic  13.5 us (5%)
    all_gather x1, waiting for transfers between devices, shards(): piece = lax.all_gather(flat, 'band', axis=0, tiled=True)  114 us
    psum x1, blocking collectives, shards(): over_sum, proj_sum = lax.psum((over_rows, proj_rows), 'domain')  27.6 us
    ppermute x6, starting transfers between devices, partner(): lax.ppermute(x, axis, [(i, i ^ 1 << apart) for i in range(lax.axis_size(a...  24.2 us
    ppermute x6, starting transfers between devices, from_behind(): return lax.ppermute(value, axis, pairs)  20.2 us
    dot_general x2, matrix products, contract(): lax.dot_general(left, right, (((1,), (1,)), ((), ())), precision=lax.Prec...  15.7 us
    unnamed x14, local copies, waits for them, and re-layouts  11.9 us
    ppermute x6, waiting for transfers between devices, partner(): lax.ppermute(x, axis, [(i, i ^ 1 << apart) for i in range(lax.axis_size(a...  11.9 us
    div x1, other arithmetic, shards(): first = (hamiltonian(start, grid_pot) - filter_center * start) / filter_half  7.69 us
  transfers between devices with their start and end apart: 13, of which 4 were waited for; matrix products, arithmetic and copies ran while one was open for 3% of the time, Pallas kernels for 0%

commit v1 on v0

v1 whole, which is shorter than its diff:
```python
import functools

import jax
import jax.numpy as jnp
from jax import lax
from jax.experimental import pallas as pl
from jax.experimental.pallas import tpu as pltpu
from jax.sharding import PartitionSpec as P

second_coeffs = (
    -5369.0 / 1800.0,
    12.0 / 7.0,
    -15.0 / 56.0,
    10.0 / 189.0,
    -1.0 / 112.0,
    2.0 / 1925.0,
    -1.0 / 16632.0,
)
filter_center = 6.5
filter_half = 5.5
reach = 6
MESH = pl.DeviceIdType.MESH

CX, CY, CZ = 16, 16, 128
NY = 32
NB = 64
NCELL = 524288


def hamiltonian(src, j, beside, pot, lane):
    here = src[j]
    total = (-1.5 * second_coeffs[0] + pot) * here
    for s in range(1, reach + 1):
        pair = src[j + s] + src[j - s]
        pair = pair + (pltpu.roll(here, s, 0) + pltpu.roll(here, NY - s, 0))
        ahead = pltpu.roll(jnp.where(lane < s, beside, here), CZ - s, 1)
        behind = pltpu.roll(jnp.where(lane >= CZ - s, beside, here), s, 1)
        total = total + (-0.5 * second_coeffs[s]) * (pair + (ahead + behind))
    return total


def kernel(
    orb_in, pot_in, out_f, out_s, out_p,
    orb, pot, first, fil, zo, zf, zs, hf, gf, gh, part, r1, r2, tot,
    loc_sem, in_send, in_recv, core_send, core_recv, x_send, x_recv,
    a2a_send, a2a_recv, back_send, back_recv, red_send, red_recv,
):
    band = lax.axis_index("band")
    domain = lax.axis_index("domain")
    z, yh = band // 4, band % 4
    x, yl, core = domain // 4, (domain // 2) % 2, domain % 2
    y = yh * 2 + yl
    zy = z * 8 + y
    mine = pl.multiple_of(yl * CY, CY)
    other = pl.multiple_of((1 - yl) * CY, CY)

    def at(pz, py, px, pc):
        return (pz * 4 + py // 2, px * 4 + (py % 2) * 2 + pc)

    xn, xp = (x + 1) % 4, (x + 3) % 4
    yo = y + 1 - 2 * yl
    yq = (y + 7 + 2 * yl) % 8
    mate = at(z, y, x, 1 - core)

    def rdma(src, dst, send, recv, to):
        return pltpu.make_async_remote_copy(
            src_ref=src, dst_ref=dst, send_sem=send, recv_sem=recv,
            device_id=to, device_id_type=MESH,
        )

    local = [
        pltpu.make_async_copy(orb_in.at[yl], orb.at[pl.ds(12, CX), pl.ds(mine, CY)], loc_sem.at[0]),
        pltpu.make_async_copy(pot_in, pot.at[pl.ds(6, CX), pl.ds(mine, CY)], loc_sem.at[1]),
    ]
    for c in local:
        c.start()

    bar = pltpu.get_barrier_semaphore()

    def hello(to):
        pl.semaphore_signal(bar, inc=1, device_id=to, device_id_type=MESH)

    for px in (xn, xp):
        hello(at(z, yo, px, core))
        hello(at(z, yq, px, core))

    def hello_near(j, _):
        hello(((z * 4 + (yh ^ (j >> 3))), (x ^ ((j >> 1) & 3)) * 4 + yl * 2 + (core ^ (j & 1))))
        return 0

    def hello_plane(j, _):
        a, kz = j >> 3, j & 7
        hello(at(z ^ kz, y ^ (a ^ kz), x, core))
        return 0

    lax.fori_loop(1, 2, hello_near, 0)
    lax.fori_loop(2, 8, hello_near, 0)
    for k in (1, 2, 3):
        lax.fori_loop(k * 8 + 1, k * 8 + 8, hello_near, 0)
    lax.fori_loop(1, 64, hello_plane, 0)
    pl.semaphore_wait(bar, 4 + 28 + 63)

    rows = pl.ds(mine, CY)
    entry = [
        rdma(orb_in.at[1 - yl], orb.at[pl.ds(12, CX), rows], in_send.at[0], in_recv.at[0], at(z, yo, x, core)),
        rdma(orb_in.at[1 - yl, pl.ds(4, 12)], orb.at[pl.ds(0, 12), rows], in_send.at[1], in_recv.at[1], at(z, yo, xn, core)),
        rdma(orb_in.at[1 - yl, pl.ds(0, 12)], orb.at[pl.ds(28, 12), rows], in_send.at[2], in_recv.at[2], at(z, yo, xp, core)),
        rdma(orb_in.at[yl, pl.ds(4, 12)], orb.at[pl.ds(0, 12), rows], in_send.at[3], in_recv.at[3], at(z, y, xn, core)),
        rdma(orb_in.at[yl, pl.ds(0, 12)], orb.at[pl.ds(28, 12), rows], in_send.at[4], in_recv.at[4], at(z, y, xp, core)),
        rdma(pot_in, pot.at[pl.ds(6, CX), rows], in_send.at[5], in_recv.at[5], at(z, yq, x, core)),
        rdma(pot_in.at[pl.ds(10, 6)], pot.at[pl.ds(0, 6), rows], in_send.at[6], in_recv.at[6], at(z, yq, xn, core)),
        rdma(pot_in.at[pl.ds(0, 6)], pot.at[pl.ds(22, 6), rows], in_send.at[7], in_recv.at[7], at(z, yq, xp, core)),
        rdma(pot_in.at[pl.ds(10, 6)], pot.at[pl.ds(0, 6), rows], in_send.at[8], in_recv.at[8], at(z, y, xn, core)),
        rdma(pot_in.at[pl.ds(0, 6)], pot.at[pl.ds(22, 6), rows], in_send.at[9], in_recv.at[9], at(z, y, xp, core)),
    ]
    for c in entry:
        c.start()
    for c in local:
        c.wait()

    def to_mate(k, src, dst):
        c = rdma(src, dst, core_send.at[k], core_recv.at[k], mate)
        c.start()
        return c

    beside = [to_mate(0, orb.at[pl.ds(12, CX), pl.ds(mine, CY)], zo.at[pl.ds(6, CX), pl.ds(mine, CY)])]
    entry[0].wait_recv()
    beside.append(to_mate(1, orb.at[pl.ds(12, CX), pl.ds(other, CY)], zo.at[pl.ds(6, CX), pl.ds(other, CY)]))
    entry[1].wait_recv()
    entry[3].wait_recv()
    beside.append(to_mate(2, orb.at[pl.ds(6, 6)], zo.at[pl.ds(0, 6)]))
    entry[2].wait_recv()
    entry[4].wait_recv()
    beside.append(to_mate(3, orb.at[pl.ds(28, 6)], zo.at[pl.ds(22, 6)]))
    for c in entry[5:]:
        c.wait_recv()
    for c in beside:
        c.wait_recv()

    lane = lax.broadcasted_iota(jnp.int32, (NY, CZ), 1)

    def step_first(k, _):
        h = hamiltonian(orb, k + 6, zo[k], pot[k] - filter_center, lane)
        first[k] = h * (1.0 / filter_half)
        return 0

    lax.fori_loop(0, CX + 12, step_first, 0)

    mid = pl.ds(6, CX)
    beside.append(to_mate(4, first.at[mid], zf))
    beside[4].wait_recv()

    def step_filtered(k, _):
        h = hamiltonian(first, k + 6, zf[k], pot[k + 6] - filter_center, lane)
        fil[k + 6] = h * (2.0 / filter_half) - orb[k + 12]
        return 0

    lax.fori_loop(0, CX, step_filtered, 0)

    rims = [
        rdma(fil.at[pl.ds(6, 6)], fil.at[pl.ds(22, 6)], x_send.at[0], x_recv.at[0], at(z, y, xp, core)),
        rdma(fil.at[pl.ds(16, 6)], fil.at[pl.ds(0, 6)], x_send.at[1], x_recv.at[1], at(z, y, xn, core)),
    ]
    for c in rims:
        c.start()
    beside.append(to_mate(5, fil.at[mid], zs))

    def spread(src, low, got, which):
        def send(j, _):
            a, kz = j >> 3, j & 7
            pz, py = z ^ kz, y ^ (a ^ kz)
            row = pl.multiple_of((py % 4) * 8, 8)
            rdma(
                src.at[low + pz * 2 + py // 4, pl.ds(row, 8)], got.at[zy],
                a2a_send.at[which], a2a_recv.at[which], at(pz, py, x, core),
            ).start()
            return 0

        lax.fori_loop(1, 64, send, 0)
        got[zy] = src[low + zy // 4, pl.ds(pl.multiple_of((zy % 4) * 8, 8), 8)]

    def spread_all(got, which):
        return rdma(got.at[pl.ds(0, 63)], got.at[pl.ds(0, 63)], a2a_send.at[which], a2a_recv.at[which], mate)

    spread(fil, 6, gf, 0)

    for c in rims:
        c.wait_recv()
    beside[5].wait_recv()

    def step_applied(k, _):
        hf[k] = hamiltonian(fil, k + 6, zs[k], pot[k + 6], lane)
        return 0

    lax.fori_loop(0, CX, step_applied, 0)
    spread(hf, 0, gh, 1)

    back = rdma(fil.at[mid, pl.ds(other, CY)], out_f.at[yl], back_send, back_recv, at(z, yo, x, core))
    back.start()
    keep = pltpu.make_async_copy(fil.at[mid, pl.ds(mine, CY)], out_f.at[yl], loc_sem.at[2])
    keep.start()

    def contract(left, right):
        return lax.dot_general(
            left, right, (((1,), (1,)), ((), ())),
            precision=lax.Precision.HIGHEST, preferred_element_type=jnp.float32,
        )

    spread_all(gf, 0).wait_recv()
    spread_all(gh, 1).wait_recv()
    both = jnp.zeros((NB, 2 * NB), jnp.float32)
    for s in range(8):
        left = gf[:, s, :]
        both = both + contract(left, jnp.concatenate([left, gh[:, s, :]], axis=0))
    part[...] = both.reshape(8, 8, 2 * NB)

    slot = z * 2 + yl

    def send_rows(j, _):
        pz, pl_ = z ^ (j >> 1), yl ^ (j & 1)
        rdma(
            part.at[pz], r1.at[slot], red_send.at[0], red_recv.at[0],
            (pz * 4 + yh, x * 4 + pl_ * 2 + core),
        ).start()
        return 0

    lax.fori_loop(1, 16, send_rows, 0)
    r1[slot] = part[z]
    red1 = rdma(r1.at[pl.ds(0, 15)], r1.at[pl.ds(0, 15)], red_send.at[0], red_recv.at[0], mate)
    red1.wait_recv()
    tot[...] = jnp.sum(r1[...], axis=0)

    slot2 = yh * 8 + x * 2 + core

    def send_total(j, _):
        rdma(
            tot, r2.at[slot2], red_send.at[1], red_recv.at[1],
            (z * 4 + (yh ^ (j >> 3)), (x ^ ((j >> 1) & 3)) * 4 + yl * 2 + (core ^ (j & 1))),
        ).start()
        return 0

    lax.fori_loop(1, 32, send_total, 0)
    r2[slot2] = tot[...]
    red2 = rdma(r2.at[pl.ds(0, 31)], r2.at[pl.ds(0, 31)], red_send.at[1], red_recv.at[1], mate)
    red2.wait_recv()
    r1[0] = jnp.sum(r2[...], axis=0) * (1.0 / NCELL)
    rows = r1[0, pl.ds(yh * 2, 2), :]
    out_s[...] = rows[:, :NB]
    out_p[...] = rows[:, NB:]

    for c in entry:
        c.wait_send()
    for c in beside:
        c.wait_send()
    for c in rims:
        c.wait_send()
    spread_all(gf, 0).wait_send()
    spread_all(gh, 1).wait_send()
    red1.wait_send()
    red2.wait_send()
    keep.wait()
    back.wait()


def shards(orbitals, potential):
    f32 = jnp.float32
    vmem = pltpu.VMEM
    dma = pltpu.SemaphoreType.DMA
    any_ = pl.BlockSpec(memory_space=pl.ANY)
    full = pl.BlockSpec(memory_space=pltpu.VMEM)
    filtered, inter, proj = pl.pallas_call(
        kernel,
        out_shape=(
            jax.ShapeDtypeStruct((2, CX, CY, CZ), f32),
            jax.ShapeDtypeStruct((2, NB), f32),
            jax.ShapeDtypeStruct((2, NB), f32),
        ),
        in_specs=[any_, any_],
        out_specs=(any_, full, full),
        scratch_shapes=[
            vmem((CX + 24, NY, CZ), f32),
            vmem((CX + 12, NY, CZ), f32),
            vmem((CX + 12, NY, CZ), f32),
            vmem((CX + 12, NY, CZ), f32),
            vmem((CX + 12, NY, CZ), f32),
            vmem((CX, NY, CZ), f32),
            vmem((CX, NY, CZ), f32),
            vmem((CX, NY, CZ), f32),
            vmem((NB, 8, CZ), f32),
            vmem((NB, 8, CZ), f32),
            vmem((8, 8, 2 * NB), f32),
            vmem((16, 8, 2 * NB), f32),
            vmem((32, 8, 2 * NB), f32),
            vmem((8, 2 * NB), f32),
            dma((3,)), dma((10,)), dma((10,)), dma((6,)), dma((6,)), dma((2,)), dma((2,)),
            dma((2,)), dma((2,)), dma, dma, dma((2,)), dma((2,)),
        ],
        compiler_params=pltpu.CompilerParams(
            collective_id=0, has_side_effects=True, vmem_limit_bytes=32 << 20
        ),
        name="chebyshev_step",
    )(orbitals.reshape(2, CX, CY, CZ), potential.reshape(CX, CY, CZ))
    return filtered[:, None], inter, proj


def solution(mesh):
    return jax.shard_map(
        shards,
        mesh=mesh,
        in_specs=(P("band", "domain", None, None, None), P("domain", None, None, None)),
        out_specs=(P("band", "domain", None, None, None), P("band", None), P("band", None)),
        check_vma=False,
    )
```

time: 263 us -> 70.9 us (0.27)
  waiting for transfers between devices: 126 us -> 0 us
  Pallas kernels: 0 us -> 66.4 us
  starting transfers between devices: 44.4 us -> 0 us
  blocking collectives: 27.6 us -> 0 us
  matrix products: 15.7 us -> 0 us
  local copies, waits for them, and re-layouts: 18.9 us -> 3.68 us
  between operations: 14.5 us -> 0.65 us
  other arithmetic: 13.5 us -> 0 us
    all_gather x1 -> x0, waiting for transfers between devices: 114 us -> none  [shards(): piece = lax.all_gather(flat, 'band', axis=0, tiled=True)]
    pallas_call x0 -> x1, Pallas kernels: none -> 66.4 us  [shards(): pl.pallas_call(kernel, out_shape=(jax.ShapeDtypeStruct((2, CX, CY, CZ), f...]
    ppermute x12 -> x0, starting transfers between devices: 44.4 us -> none  [the longest x6 24.2 us: partner(): lax.ppermute(x, axis, [(i, i ^ 1 << apart) for i in range(lax.axis_size(a...]
    psum x1 -> x0, blocking collectives: 27.6 us -> none  [shards(): over_sum, proj_sum = lax.psum((over_rows, proj_rows), 'domain')]
    dot_general x2 -> x0, matrix products: 15.7 us -> none  [contract(): lax.dot_general(left, right, (((1,), (1,)), ((), ())), precision=lax.Prec...]
    ppermute x12 -> x0, waiting for transfers between devices: 12.1 us -> none  [the longest x6 11.9 us: partner(): lax.ppermute(x, axis, [(i, i ^ 1 << apart) for i in range(lax.axis_size(a...]
    div x3 -> x0, other arithmetic: 8.82 us -> none  [the longest x1 7.69 us: shards(): first = (hamiltonian(start, grid_pot) - filter_center * start) / filter_half]
    unnamed x14 -> x7, local copies, waits for them, and re-layouts: 11.9 us -> 3.68 us
  transfers between devices with their start and end apart: 13 -> 0, of which waited for: 4 -> 0; matrix products, arithmetic and copies ran while one was open for 3% -> 0% of each run, Pallas kernels for 0% -> 0%
where the time goes in v1:
time: 70.9 us; the launch traced here: 70.7 us
  Pallas kernels  66.4 us (94%)
  local copies, waits for them, and re-layouts  3.68 us (5%)
    pallas_call x1, Pallas kernels, shards(): pl.pallas_call(kernel, out_shape=(jax.ShapeDtypeStruct((2, CX, CY, CZ), f...  66.4 us
    unnamed x7, local copies, waits for them, and re-layouts  3.68 us

profile of v1, /device:TPU:1, one launch (start us, length us, event | category | flops | bytes accessed | tf_op | source)
XLA Modules:
  0.0 70.7 jit_solution(14311403300100806722)
XLA Ops:
  0.6 0.0 copy-start
  0.6 0.9 %copy-done = f32[2,1,16,16,128]{4,3,2,1,0:T(8,128)S(1)} copy-done((f32[2,1,16,16,128]{4,3,2,1,0:T(8,128)S(1)}, f32[2,1,16,16,128]{4,3,2,1,0:T(8,128)}, u32[]{:S(2)}) %copy-start) | copy-done | bytes 262168
  1.6 0.0 copy-start.1
  1.6 0.9 %copy-done.1 = f32[1,16,16,128]{3,2,1,0:T(8,128)S(1)} copy-done((f32[1,16,16,128]{3,2,1,0:T(8,128)S(1)}, f32[1,16,16,128]{3,2,1,0:T(8,128)}, u32[]{:S(2)}) %copy-start.1) | copy-done | bytes 131096
  2.5 66.4 %chebyshev_step.1 = (f32[2,16,16,128]{3,2,1,0:T(8,128)S(1)}, f32[2,64]{1,0:T(2,128)S(1)}, f32[2,64]{1,0:T(2,128)S(1)}) custom-call(f32[2,16,16,128]{3,2,1,0:T(8,128)S(1)} %bitcast.5, f32[16,16,128]{2,1,0:T(8,128)S(1)} %bitcast.7), custom_call_target="tpu_custom_call" | custom-call | tf_op jit(solution)/shard_map/chebyshev_step/pallas_call | solution.py:271
  68.9 0.7 copy.9
  69.6 0.6 copy.10
  70.2 0.6 copy.11
Async XLA Ops:
  0.6 1.0 %copy-start = (f32[2,1,16,16,128]{4,3,2,1,0:T(8,128)S(1)}, f32[2,1,16,16,128]{4,3,2,1,0:T(8,128)}, u32[]{:S(2)}) copy-start(f32[2,1,16,16,128]{4,3,2,1,0:T(8,128)} %param.2) | copy-start | bytes 786436
  1.6 0.9 %copy-start.1 = (f32[1,16,16,128]{3,2,1,0:T(8,128)S(1)}, f32[1,16,16,128]{3,2,1,0:T(8,128)}, u32[]{:S(2)}) copy-start(f32[1,16,16,128]{3,2,1,0:T(8,128)} %param.3) | copy-start | bytes 393220

commit v2 on v1

v2 whole, which is shorter than its diff:
```python
import functools

import jax
import jax.numpy as jnp
from jax import lax
from jax.experimental import pallas as pl
from jax.experimental.pallas import tpu as pltpu
from jax.sharding import PartitionSpec as P

second_coeffs = (
    -5369.0 / 1800.0,
    12.0 / 7.0,
    -15.0 / 56.0,
    10.0 / 189.0,
    -1.0 / 112.0,
    2.0 / 1925.0,
    -1.0 / 16632.0,
)
filter_center = 6.5
filter_half = 5.5
reach = 6
MESH = pl.DeviceIdType.MESH

CX, CY, CZ = 16, 16, 128
NY = 32
NB = 64
NCELL = 524288


def part_y(here, pot):
    total = (-1.5 * second_coeffs[0] + pot) * here
    for s in range(1, reach + 1):
        pair = pltpu.roll(here, s, 0) + pltpu.roll(here, NY - s, 0)
        total = total + (-0.5 * second_coeffs[s]) * pair
    return total


def part_z(here, beside, lane):
    total = None
    for s in range(1, reach + 1):
        ahead = pltpu.roll(jnp.where(lane < s, beside, here), CZ - s, 1)
        behind = pltpu.roll(jnp.where(lane >= CZ - s, beside, here), s, 1)
        term = (-0.5 * second_coeffs[s]) * (ahead + behind)
        total = term if total is None else total + term
    return total


def part_x(src, j):
    total = None
    for s in range(1, reach + 1):
        term = (-0.5 * second_coeffs[s]) * (src[j + s] + src[j - s])
        total = term if total is None else total + term
    return total


def far_first(i, half):
    return half + ((i + 1) // 2) * (2 * (i % 2) - 1)


def kernel(
    orb_in, pot_in, out_f, out_s, out_p,
    orb, pot, first, fil, zo, zf, zs, acc, hf, gf, gh, part, r1, r2, tot,
    loc_sem, in_send, in_recv, core_send, core_recv, x_send, x_recv,
    a2a_send, a2a_recv, back_send, back_recv, red_send, red_recv,
):
    band = lax.axis_index("band")
    domain = lax.axis_index("domain")
    z, yh = band // 4, band % 4
    x, yl, core = domain // 4, (domain // 2) % 2, domain % 2
    y = yh * 2 + yl
    zy = z * 8 + y
    mine = pl.multiple_of(yl * CY, CY)
    other = pl.multiple_of((1 - yl) * CY, CY)

    def at(pz, py, px, pc):
        return (pz * 4 + py // 2, px * 4 + (py % 2) * 2 + pc)

    xn, xp = (x + 1) % 4, (x + 3) % 4
    yo = y + 1 - 2 * yl
    yq = (y + 7 + 2 * yl) % 8
    mate = at(z, y, x, 1 - core)
    to_xn, to_xp = at(z, y, xn, core), at(z, y, xp, core)

    def rdma(src, dst, send, recv, to):
        return pltpu.make_async_remote_copy(
            src_ref=src, dst_ref=dst, send_sem=send, recv_sem=recv,
            device_id=to, device_id_type=MESH,
        )

    mid = pl.ds(6, CX)
    low, high = pl.ds(0, 6), pl.ds(22, 6)
    rows = pl.ds(mine, CY)
    rows_other = pl.ds(other, CY)

    local = [
        pltpu.make_async_copy(orb_in.at[yl], orb.at[mid, rows], loc_sem.at[0]),
        pltpu.make_async_copy(pot_in, pot.at[:, rows], loc_sem.at[1]),
    ]
    for c in local:
        c.start()

    bar = pltpu.get_barrier_semaphore()

    def hello(to):
        pl.semaphore_signal(bar, inc=1, device_id=to, device_id_type=MESH)

    hello(at(z, yo, xn, core))
    hello(at(z, yo, xp, core))

    def hello_near(j, _):
        hello(((z * 4 + (yh ^ (j >> 3))), (x ^ ((j >> 1) & 3)) * 4 + yl * 2 + (core ^ (j & 1))))
        return 0

    def hello_plane(j, _):
        a, kz = j >> 3, j & 7
        hello(at(z ^ kz, y ^ (a ^ kz), x, core))
        return 0

    lax.fori_loop(1, 8, hello_near, 0)
    for k in (1, 2, 3):
        lax.fori_loop(k * 8 + 1, k * 8 + 8, hello_near, 0)
    lax.fori_loop(1, 64, hello_plane, 0)
    pl.semaphore_wait(bar, 2 + 28 + 63)

    entry = [
        rdma(orb_in.at[1 - yl], orb.at[mid, rows], in_send.at[0], in_recv.at[0], at(z, yo, x, core)),
        rdma(orb_in.at[1 - yl, pl.ds(10, 6)], orb.at[low, rows], in_send.at[1], in_recv.at[1], at(z, yo, xn, core)),
        rdma(orb_in.at[1 - yl, pl.ds(0, 6)], orb.at[high, rows], in_send.at[2], in_recv.at[2], at(z, yo, xp, core)),
        rdma(orb_in.at[yl, pl.ds(10, 6)], orb.at[low, rows], in_send.at[3], in_recv.at[3], to_xn),
        rdma(orb_in.at[yl, pl.ds(0, 6)], orb.at[high, rows], in_send.at[4], in_recv.at[4], to_xp),
        rdma(pot_in, pot.at[:, rows], in_send.at[5], in_recv.at[5], at(z, yq, x, core)),
    ]

    def to_mate(k, src, dst):
        c = rdma(src, dst, core_send.at[k], core_recv.at[k], mate)
        c.start()
        return c

    beside = [to_mate(0, orb_in.at[yl], zo.at[:, rows])]
    for c in entry:
        c.start()
    for c in local:
        c.wait()
    entry[0].wait_recv()
    beside.append(to_mate(1, orb.at[mid, rows_other], zo.at[:, rows_other]))
    entry[5].wait_recv()

    lane = lax.broadcasted_iota(jnp.int32, (NY, CZ), 1)

    def over_layers(body):
        def step(k, _):
            body(k)
            return 0

        lax.fori_loop(0, CX, step, 0)

    def along_y(src):
        def body(k):
            acc[k] = part_y(src[k + 6], pot[k])

        return body

    def along_z(src, beside_src):
        def body(k):
            acc[k] = acc[k] + part_z(src[k + 6], beside_src[k], lane)

        return body

    def rims_of(src, k):
        cs = [
            rdma(src.at[pl.ds(6, 6)], src.at[high], x_send.at[k], x_recv.at[k], to_xp),
            rdma(src.at[pl.ds(16, 6)], src.at[low], x_send.at[k + 1], x_recv.at[k + 1], to_xn),
        ]
        for c in cs:
            c.start()
        return cs

    over_layers(along_y(orb))
    beside[0].wait_recv()
    beside[1].wait_recv()
    over_layers(along_z(orb, zo))
    for c in entry[1:5]:
        c.wait_recv()

    def last_first(k):
        here = orb[k + 6]
        h = acc[k] + part_x(orb, k + 6)
        first[k + 6] = (h - filter_center * here) * (1.0 / filter_half)

    over_layers(last_first)

    rims = rims_of(first, 0)
    beside.append(to_mate(2, first.at[mid], zf))
    over_layers(along_y(first))
    beside[2].wait_recv()
    over_layers(along_z(first, zf))
    for c in rims:
        c.wait_recv()

    def last_filtered(k):
        here = first[k + 6]
        h = acc[k] + part_x(first, k + 6)
        fil[k + 6] = (h - filter_center * here) * (2.0 / filter_half) - orb[k + 6]

    over_layers(last_filtered)

    rims += rims_of(fil, 2)
    beside.append(to_mate(3, fil.at[mid], zs))

    def turn(j):
        pz = (z + far_first(j // 2, 4)) % 8
        return pz, (y // 4 + 1 + j) % 2

    def send_tiles(src, skip, got, which, pz, py_half, count):
        for i in range(count):
            py = py_half * 4 + (y + 1 + i) % 4
            rdma(
                src.at[skip + pz * 2 + py_half, pl.ds(pl.multiple_of((py % 4) * 8, 8), 8)], got.at[zy],
                a2a_send.at[which], a2a_recv.at[which], at(pz, py, x, core),
            ).start()

    def keep_tile(src, skip, got):
        got[zy] = src[skip + zy // 4, pl.ds(pl.multiple_of((zy % 4) * 8, 8), 8)]

    def all_tiles(got, which):
        return rdma(got.at[pl.ds(0, 63)], got.at[pl.ds(0, 63)], a2a_send.at[which], a2a_recv.at[which], mate)

    def filtered_out(j, _):
        pz, half = turn(j)
        send_tiles(fil, 6, gf, 0, pz, half, 4)
        acc[j] = part_y(fil[j + 6], pot[j])
        return 0

    lax.fori_loop(0, CX - 1, filtered_out, 0)
    send_tiles(fil, 6, gf, 0, z, y // 4, 3)
    keep_tile(fil, 6, gf)
    acc[CX - 1] = part_y(fil[CX + 5], pot[CX - 1])

    beside[3].wait_recv()
    over_layers(along_z(fil, zs))
    for c in rims[2:]:
        c.wait_recv()

    def applied_layer(k):
        hf[k] = acc[k] + part_x(fil, k + 6)

    def applied_out(j, _):
        pz, half = turn(j)
        applied_layer(pz * 2 + half)
        send_tiles(hf, 0, gh, 1, pz, half, 4)
        return 0

    lax.fori_loop(0, CX - 1, applied_out, 0)
    applied_layer(zy // 4)
    send_tiles(hf, 0, gh, 1, z, y // 4, 3)
    keep_tile(hf, 0, gh)

    def contract(left, right):
        return lax.dot_general(
            left, right, (((1,), (1,)), ((), ())),
            precision=lax.Precision.HIGHEST, preferred_element_type=jnp.float32,
        )

    all_tiles(gf, 0).wait_recv()
    all_tiles(gh, 1).wait_recv()

    back = rdma(fil.at[mid, rows_other], out_f.at[yl], back_send, back_recv, at(z, yo, x, core))
    back.start()
    keep = pltpu.make_async_copy(fil.at[mid, rows], out_f.at[yl], loc_sem.at[2])
    keep.start()

    both = jnp.zeros((NB, 2 * NB), jnp.float32)
    for s in range(8):
        left = gf[:, s, :]
        both = both + contract(left, jnp.concatenate([left, gh[:, s, :]], axis=0))
    part[...] = both.reshape(8, 8, 2 * NB)

    slot = z * 2 + yl

    def send_rows(j, _):
        pz, py = (z + far_first(j // 2, 4)) % 8, (yl + 1 + j) % 2
        rdma(
            part.at[pz], r1.at[slot], red_send.at[0], red_recv.at[0],
            (pz * 4 + yh, x * 4 + py * 2 + core),
        ).start()
        return 0

    lax.fori_loop(0, 15, send_rows, 0)
    r1[slot] = part[z]
    red1 = rdma(r1.at[pl.ds(0, 15)], r1.at[pl.ds(0, 15)], red_send.at[0], red_recv.at[0], mate)
    red1.wait_recv()

    total = jnp.sum(r1[...], axis=0)
    for i in range(4):
        tot[i] = total[2 * i : 2 * i + 2]
    slot2 = yh * 8 + x * 2 + core

    def send_total(j, _):
        ph, px = (yh + far_first(j // 8, 2)) % 4, (x + far_first((j // 2) % 4, 2)) % 4
        rdma(
            tot.at[ph], r2.at[slot2], red_send.at[1], red_recv.at[1],
            (z * 4 + ph, px * 4 + yl * 2 + (core + 1 + j) % 2),
        ).start()
        return 0

    lax.fori_loop(0, 31, send_total, 0)
    r2[slot2] = tot[yh]
    red2 = rdma(r2.at[pl.ds(0, 31)], r2.at[pl.ds(0, 31)], red_send.at[1], red_recv.at[1], mate)
    red2.wait_recv()
    result = jnp.sum(r2[...], axis=0) * (1.0 / NCELL)
    out_s[...] = result[:, :NB]
    out_p[...] = result[:, NB:]

    for c in entry:
        c.wait_send()
    for c in beside:
        c.wait_send()
    for c in rims:
        c.wait_send()
    all_tiles(gf, 0).wait_send()
    all_tiles(gh, 1).wait_send()
    red1.wait_send()
    red2.wait_send()
    keep.wait()
    back.wait()


def shards(orbitals, potential):
    f32 = jnp.float32
    vmem = pltpu.VMEM
    dma = pltpu.SemaphoreType.DMA
    hbm = pl.BlockSpec(memory_space=pltpu.HBM)
    full = pl.BlockSpec(memory_space=pltpu.VMEM)
    filtered, inter, proj = pl.pallas_call(
        kernel,
        out_shape=(
            jax.ShapeDtypeStruct((2, CX, CY, CZ), f32),
            jax.ShapeDtypeStruct((2, NB), f32),
            jax.ShapeDtypeStruct((2, NB), f32),
        ),
        in_specs=[hbm, hbm],
        out_specs=(hbm, full, full),
        scratch_shapes=[
            vmem((CX + 12, NY, CZ), f32),
            vmem((CX, NY, CZ), f32),
            vmem((CX + 12, NY, CZ), f32),
            vmem((CX + 12, NY, CZ), f32),
            vmem((CX, NY, CZ), f32),
            vmem((CX, NY, CZ), f32),
            vmem((CX, NY, CZ), f32),
            vmem((CX, NY, CZ), f32),
            vmem((CX, NY, CZ), f32),
            vmem((NB, 8, CZ), f32),
            vmem((NB, 8, CZ), f32),
            vmem((8, 8, 2 * NB), f32),
            vmem((16, 8, 2 * NB), f32),
            vmem((32, 2, 2 * NB), f32),
            vmem((4, 2, 2 * NB), f32),
            dma((3,)), dma((6,)), dma((6,)), dma((4,)), dma((4,)), dma((4,)), dma((4,)),
            dma((2,)), dma((2,)), dma, dma, dma((2,)), dma((2,)),
        ],
        compiler_params=pltpu.CompilerParams(
            collective_id=0, has_side_effects=True, vmem_limit_bytes=60 << 20
        ),
        name="chebyshev_step",
    )(orbitals.reshape(2, CX, CY, CZ), potential.reshape(CX, CY, CZ))
    return filtered[:, None], inter, proj


def solution(mesh):
    return jax.shard_map(
        shards,
        mesh=mesh,
        in_specs=(P("band", "domain", None, None, None), P("domain", None, None, None)),
        out_specs=(P("band", "domain", None, None, None), P("band", None), P("band", None)),
        check_vma=False,
    )
```

time: 70.9 us -> 65.2 us (0.920)
  Pallas kernels: 66.4 us -> 61.5 us
  local copies, waits for them, and re-layouts: 3.68 us -> 2.91 us
    pallas_call x1, Pallas kernels: 66.4 us -> 61.5 us  [shards(): pl.pallas_call(kernel, out_shape=(jax.ShapeDtypeStruct((2, CX, CY, CZ), f...]
    unnamed x7, local copies, waits for them, and re-layouts: 3.68 us -> 2.91 us
where the time goes in v2:
time: 65.2 us; the launch traced here: 65.1 us
  Pallas kernels  61.5 us (94%)
  local copies, waits for them, and re-layouts  2.91 us (4%)
    pallas_call x1, Pallas kernels, shards(): pl.pallas_call(kernel, out_shape=(jax.ShapeDtypeStruct((2, CX, CY, CZ), f...  61.5 us
    unnamed x7, local copies, waits for them, and re-layouts  2.91 us

profile of v2, /device:TPU:1, one launch (start us, length us, event | category | flops | bytes accessed | tf_op | source)
XLA Modules:
  0.0 65.1 jit_solution(3588447925460283166)
XLA Ops:
  0.6 61.5 %chebyshev_step.1 = (f32[2,16,16,128]{3,2,1,0:T(8,128)}, f32[2,64]{1,0:T(2,128)}, f32[2,64]{1,0:T(2,128)}) custom-call(f32[2,16,16,128]{3,2,1,0:T(8,128)} %bitcast.5, f32[16,16,128]{2,1,0:T(8,128)} %bitcast.7), custom_call_target="tpu_custom_call" | custom-call | tf_op jit(solution)/shard_map/chebyshev_step/pallas_call | solution.py:334
  62.2 0.0 copy-start.1
  62.2 1.7 %copy.9 = f32[2,1,16,16,128]{4,3,2,1,0:T(8,128)} copy(f32[2,1,16,16,128]{4,3,2,1,0:T(8,128)} %bitcast.6) | data formatting | bytes 524288
  63.8 0.0 copy-done.1
  63.8 0.0 copy-start
  63.8 0.6 copy.10
  64.4 0.1 copy-done
  64.5 0.6 copy.11
Async XLA Ops:
  62.2 1.7 %copy-start.1 = (f32[2,64]{1,0:T(2,128)S(1)}, f32[2,64]{1,0:T(2,128)}, u32[]{:S(2)}) copy-start(f32[2,64]{1,0:T(2,128)} %get-tuple-element.16) | copy-start | bytes 1540
  63.8 0.7 %copy-start = (f32[2,64]{1,0:T(2,128)S(1)}, f32[2,64]{1,0:T(2,128)}, u32[]{:S(2)}) copy-start(f32[2,64]{1,0:T(2,128)} %get-tuple-element.17) | copy-start | bytes 1540

commit v3 on v2

--- a/solution.py
+++ b/solution.py
@@ -27,8 +27,8 @@
 NCELL = 524288
 
 
-def part_y(here, pot):
-    total = (-1.5 * second_coeffs[0] + pot) * here
+def part_y(here):
+    total = (-1.5 * second_coeffs[0]) * here
     for s in range(1, reach + 1):
         pair = pltpu.roll(here, s, 0) + pltpu.roll(here, NY - s, 0)
         total = total + (-0.5 * second_coeffs[s]) * pair
@@ -58,10 +58,10 @@
 
 
 def kernel(
-    orb_in, pot_in, out_f, out_s, out_p,
+    orb_in, pot_in, out_f, out_sp,
     orb, pot, first, fil, zo, zf, zs, acc, hf, gf, gh, part, r1, r2, tot,
     loc_sem, in_send, in_recv, core_send, core_recv, x_send, x_recv,
-    a2a_send, a2a_recv, back_send, back_recv, red_send, red_recv,
+    a2a_send, a2a_recv, back_send, back_recv, red_send, red_recv, ring,
 ):
     band = lax.axis_index("band")
     domain = lax.axis_index("domain")
@@ -100,36 +100,37 @@
         c.start()
 
     bar = pltpu.get_barrier_semaphore()
-
-    def hello(to):
+    up_z, down_z = at((z + 1) % 8, y, x, core), at((z + 7) % 8, y, x, core)
+    up_y, down_y = at(z, (y + 1) % 8, x, core), at(z, (y + 7) % 8, x, core)
+    for to in (up_y, down_y, to_xn, to_xp, up_z, down_z, mate):
         pl.semaphore_signal(bar, inc=1, device_id=to, device_id_type=MESH)
-
-    hello(at(z, yo, xn, core))
-    hello(at(z, yo, xp, core))
-
-    def hello_near(j, _):
-        hello(((z * 4 + (yh ^ (j >> 3))), (x ^ ((j >> 1) & 3)) * 4 + yl * 2 + (core ^ (j & 1))))
-        return 0
-
-    def hello_plane(j, _):
-        a, kz = j >> 3, j & 7
-        hello(at(z ^ kz, y ^ (a ^ kz), x, core))
-        return 0
-
-    lax.fori_loop(1, 8, hello_near, 0)
-    for k in (1, 2, 3):
-        lax.fori_loop(k * 8 + 1, k * 8 + 8, hello_near, 0)
-    lax.fori_loop(1, 64, hello_plane, 0)
-    pl.semaphore_wait(bar, 2 + 28 + 63)
-
-    entry = [
-        rdma(orb_in.at[1 - yl], orb.at[mid, rows], in_send.at[0], in_recv.at[0], at(z, yo, x, core)),
-        rdma(orb_in.at[1 - yl, pl.ds(10, 6)], orb.at[low, rows], in_send.at[1], in_recv.at[1], at(z, yo, xn, core)),
-        rdma(orb_in.at[1 - yl, pl.ds(0, 6)], orb.at[high, rows], in_send.at[2], in_recv.at[2], at(z, yo, xp, core)),
+    pl.semaphore_wait(bar, 7)
+
+    far_z = (at((z + 2) % 8, y, x, core), at((z + 6) % 8, y, x, core))
+    far_y = (at(z, (y + 2) % 8, x, core), at(z, (y + 6) % 8, x, core))
+    words = (
+        (up_z, down_z), far_z, (up_y, down_y), (up_y, down_y), far_y, (mate,), (to_xn, to_xp), (to_xn, to_xp),
+    )
+
+    def tell(k):
+        for to in words[k]:
+            pl.semaphore_signal(ring.at[k], inc=1, device_id=to, device_id_type=MESH)
+
+    def hear(k):
+        pl.semaphore_wait(ring.at[k], len(words[k]))
+
+    swaps = [
+        rdma(
+            orb_in.at[1 - yl, pl.ds(k, n)], orb.at[pl.ds(k + 6, n), rows],
+            in_send.at[i], in_recv.at[i], at(z, yo, x, core),
+        )
+        for i, (k, n) in enumerate(((0, 6), (10, 6), (6, 4)))
+    ]
+    direct = [
         rdma(orb_in.at[yl, pl.ds(10, 6)], orb.at[low, rows], in_send.at[3], in_recv.at[3], to_xn),
         rdma(orb_in.at[yl, pl.ds(0, 6)], orb.at[high, rows], in_send.at[4], in_recv.at[4], to_xp),
-        rdma(pot_in, pot.at[:, rows], in_send.at[5], in_recv.at[5], at(z, yq, x, core)),
     ]
+    given = rdma(pot_in, pot.at[:, rows], in_send.at[5], in_recv.at[5], at(z, yq, x, core))
 
     def to_mate(k, src, dst):
         c = rdma(src, dst, core_send.at[k], core_recv.at[k], mate)
@@ -137,26 +138,25 @@
         return c
 
     beside = [to_mate(0, orb_in.at[yl], zo.at[:, rows])]
-    for c in entry:
+    for c in swaps + direct + [given]:
         c.start()
+    tell(0)
     for c in local:
         c.wait()
-    entry[0].wait_recv()
-    beside.append(to_mate(1, orb.at[mid, rows_other], zo.at[:, rows_other]))
-    entry[5].wait_recv()
 
     lane = lax.broadcasted_iota(jnp.int32, (NY, CZ), 1)
-
-    def over_layers(body):
+    lane_half = lax.broadcasted_iota(jnp.int32, (CY, CZ), 1)
+
+    def over_layers(body, first_layer=0, count=CX):
         def step(k, _):
             body(k)
             return 0
 
-        lax.fori_loop(0, CX, step, 0)
+        lax.fori_loop(first_layer, first_layer + count, step, 0)
 
     def along_y(src):
         def body(k):
-            acc[k] = part_y(src[k + 6], pot[k])
+            acc[k] = part_y(src[k + 6])
 
         return body
 
@@ -166,46 +166,73 @@
 
         return body
 
-    def rims_of(src, k):
-        cs = [
-            rdma(src.at[pl.ds(6, 6)], src.at[high], x_send.at[k], x_recv.at[k], to_xp),
-            rdma(src.at[pl.ds(16, 6)], src.at[low], x_send.at[k + 1], x_recv.at[k + 1], to_xn),
-        ]
-        for c in cs:
-            c.start()
-        return cs
-
+    def along_z_half(at_rows):
+        def body(k):
+            hf[k, at_rows] = part_z(orb[k + 6, at_rows], zo[k, at_rows], lane_half)
+
+        return body
+
+    def rim(src, k, to_next, at_rows=slice(None)):
+        if to_next:
+            c = rdma(src.at[pl.ds(16, 6), at_rows], src.at[low, at_rows], x_send.at[k], x_recv.at[k], to_xn)
+        else:
+            c = rdma(src.at[pl.ds(6, 6), at_rows], src.at[high, at_rows], x_send.at[k], x_recv.at[k], to_xp)
+        c.start()
+        return c
+
+    beside[0].wait_recv()
+    over_layers(along_z_half(rows))
+    hear(0)
+    tell(1)
+    swaps[0].wait_recv()
+    rims = [rim(orb, 0, False, rows_other)]
+    swaps[1].wait_recv()
+    rims.append(rim(orb, 1, True, rows_other))
+    swaps[2].wait_recv()
+    beside.append(to_mate(1, orb.at[mid, rows_other], zo.at[:, rows_other]))
     over_layers(along_y(orb))
-    beside[0].wait_recv()
+    hear(1)
+    tell(2)
     beside[1].wait_recv()
-    over_layers(along_z(orb, zo))
-    for c in entry[1:5]:
+    over_layers(along_z_half(rows_other))
+    given.wait_recv()
+    for c in direct + rims:
         c.wait_recv()
+
+    def by_edges(body, src, k):
+        over_layers(body, 0, 6)
+        sent = [rim(src, k, False)]
+        over_layers(body, 10, 6)
+        sent.append(rim(src, k + 1, True))
+        over_layers(body, 6, 4)
+        beside.append(to_mate(k // 2 + 1, src.at[mid], zf if k == 2 else zs))
+        return sent
 
     def last_first(k):
         here = orb[k + 6]
-        h = acc[k] + part_x(orb, k + 6)
-        first[k + 6] = (h - filter_center * here) * (1.0 / filter_half)
-
-    over_layers(last_first)
-
-    rims = rims_of(first, 0)
-    beside.append(to_mate(2, first.at[mid], zf))
+        h = acc[k] + hf[k] + part_x(orb, k + 6) + (pot[k] - filter_center) * here
+        first[k + 6] = h * (1.0 / filter_half)
+
+    rims += by_edges(last_first, first, 2)
+
+    hear(2)
+    tell(3)
     over_layers(along_y(first))
+    hear(3)
+    tell(4)
     beside[2].wait_recv()
     over_layers(along_z(first, zf))
-    for c in rims:
+    hear(4)
+    tell(5)
+    for c in rims[2:]:
         c.wait_recv()
 
     def last_filtered(k):
         here = first[k + 6]
-        h = acc[k] + part_x(first, k + 6)
-        fil[k + 6] = (h - filter_center * here) * (2.0 / filter_half) - orb[k + 6]
-
-    over_layers(last_filtered)
-
-    rims += rims_of(fil, 2)
-    beside.append(to_mate(3, fil.at[mid], zs))
+        h = acc[k] + part_x(first, k + 6) + (pot[k] - filter_center) * here
+        fil[k + 6] = h * (2.0 / filter_half) - orb[k + 6]
+
+    rims += by_edges(last_filtered, fil, 4)
 
     def turn(j):
         pz = (z + far_first(j // 2, 4)) % 8
@@ -228,21 +255,25 @@
     def filtered_out(j, _):
         pz, half = turn(j)
         send_tiles(fil, 6, gf, 0, pz, half, 4)
-        acc[j] = part_y(fil[j + 6], pot[j])
+        acc[j] = part_y(fil[j + 6])
         return 0
 
     lax.fori_loop(0, CX - 1, filtered_out, 0)
     send_tiles(fil, 6, gf, 0, z, y // 4, 3)
     keep_tile(fil, 6, gf)
-    acc[CX - 1] = part_y(fil[CX + 5], pot[CX - 1])
+    acc[CX - 1] = part_y(fil[CX + 5])
+    hear(5)
+    tell(6)
 
     beside[3].wait_recv()
     over_layers(along_z(fil, zs))
-    for c in rims[2:]:
+    hear(6)
+    tell(7)
+    for c in rims[4:]:
         c.wait_recv()
 
     def applied_layer(k):
-        hf[k] = acc[k] + part_x(fil, k + 6)
+        hf[k] = acc[k] + part_x(fil, k + 6) + pot[k] * fil[k + 6]
 
     def applied_out(j, _):
         pz, half = turn(j)
@@ -261,19 +292,17 @@
             precision=lax.Precision.HIGHEST, preferred_element_type=jnp.float32,
         )
 
+    hear(7)
     all_tiles(gf, 0).wait_recv()
+    over = jnp.zeros((NB, NB), jnp.float32)
+    for s in range(8):
+        over = over + contract(gf[:, s, :], gf[:, s, :])
+    part[:, :, :NB] = over.reshape(8, 8, NB)
     all_tiles(gh, 1).wait_recv()
-
-    back = rdma(fil.at[mid, rows_other], out_f.at[yl], back_send, back_recv, at(z, yo, x, core))
-    back.start()
-    keep = pltpu.make_async_copy(fil.at[mid, rows], out_f.at[yl], loc_sem.at[2])
-    keep.start()
-
-    both = jnp.zeros((NB, 2 * NB), jnp.float32)
+    proj = jnp.zeros((NB, NB), jnp.float32)
     for s in range(8):
-        left = gf[:, s, :]
-        both = both + contract(left, jnp.concatenate([left, gh[:, s, :]], axis=0))
-    part[...] = both.reshape(8, 8, 2 * NB)
+        proj = proj + contract(gf[:, s, :], gh[:, s, :])
+    part[:, :, NB:] = proj.reshape(8, 8, NB)
 
     slot = z * 2 + yl
 
@@ -286,6 +315,10 @@
         return 0
 
     lax.fori_loop(0, 15, send_rows, 0)
+    back = rdma(fil.at[mid, rows_other], out_f.at[yl], back_send, back_recv, at(z, yo, x, core))
+    back.start()
+    keep = pltpu.make_async_copy(fil.at[mid, rows], out_f.at[yl], loc_sem.at[2])
+    keep.start()
     r1[slot] = part[z]
     red1 = rdma(r1.at[pl.ds(0, 15)], r1.at[pl.ds(0, 15)], red_send.at[0], red_recv.at[0], mate)
     red1.wait_recv()
@@ -307,11 +340,9 @@
     r2[slot2] = tot[yh]
     red2 = rdma(r2.at[pl.ds(0, 31)], r2.at[pl.ds(0, 31)], red_send.at[1], red_recv.at[1], mate)
     red2.wait_recv()
-    result = jnp.sum(r2[...], axis=0) * (1.0 / NCELL)
-    out_s[...] = result[:, :NB]
-    out_p[...] = result[:, NB:]
-
-    for c in entry:
+    out_sp[...] = jnp.sum(r2[...], axis=0) * (1.0 / NCELL)
+
+    for c in swaps + direct + [given]:
         c.wait_send()
     for c in beside:
         c.wait_send()
@@ -325,21 +356,28 @@
     back.wait()
 
 
+def deliver(filtered, both, out_f, out_s, out_p, sem):
+    whole = pltpu.make_async_copy(filtered, out_f, sem)
+    whole.start()
+    out_s[...] = both[:, :NB]
+    out_p[...] = both[:, NB:]
+    whole.wait()
+
+
 def shards(orbitals, potential):
     f32 = jnp.float32
     vmem = pltpu.VMEM
     dma = pltpu.SemaphoreType.DMA
     hbm = pl.BlockSpec(memory_space=pltpu.HBM)
     full = pl.BlockSpec(memory_space=pltpu.VMEM)
-    filtered, inter, proj = pl.pallas_call(
+    filtered, both = pl.pallas_call(
         kernel,
         out_shape=(
             jax.ShapeDtypeStruct((2, CX, CY, CZ), f32),
-            jax.ShapeDtypeStruct((2, NB), f32),
-            jax.ShapeDtypeStruct((2, NB), f32),
+            jax.ShapeDtypeStruct((2, 2 * NB), f32),
         ),
         in_specs=[hbm, hbm],
-        out_specs=(hbm, full, full),
+        out_specs=(hbm, full),
         scratch_shapes=[
             vmem((CX + 12, NY, CZ), f32),
             vmem((CX, NY, CZ), f32),
@@ -356,14 +394,28 @@
             vmem((16, 8, 2 * NB), f32),
             vmem((32, 2, 2 * NB), f32),
             vmem((4, 2, 2 * NB), f32),
-            dma((3,)), dma((6,)), dma((6,)), dma((4,)), dma((4,)), dma((4,)), dma((4,)),
+            dma((3,)), dma((6,)), dma((6,)), dma((4,)), dma((4,)), dma((6,)), dma((6,)),
             dma((2,)), dma((2,)), dma, dma, dma((2,)), dma((2,)),
+            pltpu.SemaphoreType.REGULAR((8,)),
         ],
         compiler_params=pltpu.CompilerParams(
             collective_id=0, has_side_effects=True, vmem_limit_bytes=60 << 20
         ),
         name="chebyshev_step",
     )(orbitals.reshape(2, CX, CY, CZ), potential.reshape(CX, CY, CZ))
+    filtered, inter, proj = pl.pallas_call(
+        deliver,
+        out_shape=(
+            jax.ShapeDtypeStruct((2, CX, CY, CZ), f32),
+            jax.ShapeDtypeStruct((2, NB), f32),
+            jax.ShapeDtypeStruct((2, NB), f32),
+        ),
+        in_specs=[hbm, full],
+        out_specs=(hbm, full, full),
+        scratch_shapes=[dma],
+        compiler_params=pltpu.CompilerParams(vmem_limit_bytes=60 << 20),
+        name="deliver",
+    )(filtered, both)
     return filtered[:, None], inter, proj
 
 

time: 65.2 us -> 65.4 us (level)
  Pallas kernels: 61.5 us -> 64.6 us
  local copies, waits for them, and re-layouts: 2.91 us -> 0 us
    pallas_call x0 -> x1, Pallas kernels: none -> 10.3 us  [shards(): pl.pallas_call(deliver, out_shape=(jax.ShapeDtypeStruct((2, CX, CY, CZ),...]
    pallas_call x1, Pallas kernels: 61.5 us -> 54.3 us  [shards(): pl.pallas_call(kernel, out_shape=(jax.ShapeDtypeStruct((2, CX, CY, CZ), f...]
    unnamed x7 -> x0, local copies, waits for them, and re-layouts: 2.91 us -> none
where the time goes in v3:
time: 65.4 us; the launch traced here: 65.2 us
  Pallas kernels  64.6 us (99%)
    pallas_call x1, Pallas kernels, shards(): pl.pallas_call(kernel, out_shape=(jax.ShapeDtypeStruct((2, CX, CY, CZ), f...  54.3 us
    pallas_call x1, Pallas kernels, shards(): pl.pallas_call(deliver, out_shape=(jax.ShapeDtypeStruct((2, CX, CY, CZ),...  10.3 us

profile of v3, /device:TPU:1, one launch (start us, length us, event | category | flops | bytes accessed | tf_op | source)
XLA Modules:
  0.0 65.2 jit_solution(191086515696854617)
XLA Ops:
  0.6 54.3 %chebyshev_step.1 = (f32[2,16,16,128]{3,2,1,0:T(8,128)}, f32[2,128]{1,0:T(2,128)}) custom-call(f32[2,16,16,128]{3,2,1,0:T(8,128)} %bitcast.5, f32[16,16,128]{2,1,0:T(8,128)} %bitcast.6), custom_call_target="tpu_custom_call" | custom-call | tf_op jit(solution)/shard_map/chebyshev_step/pallas_call | solution.py:373
  54.9 10.3 %deliver.1 = (f32[2,16,16,128]{3,2,1,0:T(8,128)}, f32[2,64]{1,0:T(2,128)}, f32[2,64]{1,0:T(2,128)}) custom-call(f32[2,16,16,128]{3,2,1,0:T(8,128)} %get-tuple-element.8.filtered, f32[2,128]{1,0:T(2,128)} %get-tuple-element.9.both), custom_call_target="tpu_custom_call" | custom-call | tf_op jit(solution)/shard_map/deliver/pallas_call | solution.py:406

commit v4 on v3

--- a/solution.py
+++ b/solution.py
@@ -399,10 +399,13 @@
             pltpu.SemaphoreType.REGULAR((8,)),
         ],
         compiler_params=pltpu.CompilerParams(
-            collective_id=0, has_side_effects=True, vmem_limit_bytes=60 << 20
+            collective_id=0, has_side_effects=True, vmem_limit_bytes=32 << 20
         ),
         name="chebyshev_step",
-    )(orbitals.reshape(2, CX, CY, CZ), potential.reshape(CX, CY, CZ))
+    )(
+        pltpu.with_memory_space_constraint(orbitals.reshape(2, CX, CY, CZ), pltpu.HBM),
+        pltpu.with_memory_space_constraint(potential.reshape(CX, CY, CZ), pltpu.HBM),
+    )
     filtered, inter, proj = pl.pallas_call(
         deliver,
         out_shape=(
@@ -410,10 +413,10 @@
             jax.ShapeDtypeStruct((2, NB), f32),
             jax.ShapeDtypeStruct((2, NB), f32),
         ),
-        in_specs=[hbm, full],
+        in_specs=[pl.BlockSpec(memory_space=pl.ANY), full],
         out_specs=(hbm, full, full),
         scratch_shapes=[dma],
-        compiler_params=pltpu.CompilerParams(vmem_limit_bytes=60 << 20),
+        compiler_params=pltpu.CompilerParams(vmem_limit_bytes=32 << 20),
         name="deliver",
     )(filtered, both)
     return filtered[:, None], inter, proj

time: 65.4 us -> 55.8 us (0.85)
  Pallas kernels: 64.6 us -> 55 us
    pallas_call x1, Pallas kernels: 10.3 us -> 1.28 us  [shards(): pl.pallas_call(deliver, out_shape=(jax.ShapeDtypeStruct((2, CX, CY, CZ),...]
where the time goes in v4:
time: 55.8 us; the launch traced here: 55.6 us
  Pallas kernels  55 us (99%)
  between operations  0.64 us (1%)
    pallas_call x1, Pallas kernels, shards(): pl.pallas_call(kernel, out_shape=(jax.ShapeDtypeStruct((2, CX, CY, CZ), f...  53.7 us
    pallas_call x1, Pallas kernels, shards(): pl.pallas_call(deliver, out_shape=(jax.ShapeDtypeStruct((2, CX, CY, CZ),...  1.28 us

profile of v4, /device:TPU:1, one launch (start us, length us, event | category | flops | bytes accessed | tf_op | source)
XLA Modules:
  0.0 55.6 jit_solution(14960540693692608530)
XLA Ops:
  0.6 53.7 %chebyshev_step.1 = (f32[2,16,16,128]{3,2,1,0:T(8,128)S(1)}, f32[2,128]{1,0:T(2,128)S(1)}) custom-call(f32[2,16,16,128]{3,2,1,0:T(8,128)} %bitcast.5, f32[16,16,128]{2,1,0:T(8,128)} %bitcast.6), custom_call_target="tpu_custom_call" | custom-call | tf_op jit(solution)/shard_map/chebyshev_step/pallas_call | solution.py:373
  54.4 1.3 %deliver.1 = (f32[2,16,16,128]{3,2,1,0:T(8,128)}, f32[2,64]{1,0:T(2,128)}, f32[2,64]{1,0:T(2,128)}) custom-call(f32[2,16,16,128]{3,2,1,0:T(8,128)S(1)} %get-tuple-element.8.filtered, f32[2,128]{1,0:T(2,128)S(1)} %get-tuple-element.9.both), custom_call_target="tpu_custom_call" | custom-call | tf_op jit(solution)/shard_map/deliver/pallas_call | solution.py:409

commit v5 on v4

--- a/solution.py
+++ b/solution.py
@@ -58,8 +58,8 @@
 
 
 def kernel(
-    orb_in, pot_in, out_f, out_sp,
-    orb, pot, first, fil, zo, zf, zs, acc, hf, gf, gh, part, r1, r2, tot,
+    orb_in, pot_in, out_f, out_s, out_p,
+    orb, pot, first, fil, zo, zf, zs, acc, hf, gf, gh, g_high, g_low, part, r1, r2, tot,
     loc_sem, in_send, in_recv, core_send, core_recv, x_send, x_recv,
     a2a_send, a2a_recv, back_send, back_recv, red_send, red_recv, ring,
 ):
@@ -138,7 +138,7 @@
         return c
 
     beside = [to_mate(0, orb_in.at[yl], zo.at[:, rows])]
-    for c in swaps + direct + [given]:
+    for c in swaps[:2] + direct + [given]:
         c.start()
     tell(0)
     for c in local:
@@ -180,6 +180,7 @@
         c.start()
         return c
 
+    swaps[2].start()
     beside[0].wait_recv()
     over_layers(along_z_half(rows))
     hear(0)
@@ -234,34 +235,35 @@
 
     rims += by_edges(last_filtered, fil, 4)
 
-    def turn(j):
-        pz = (z + far_first(j // 2, 4)) % 8
-        return pz, (y // 4 + 1 + j) % 2
-
-    def send_tiles(src, skip, got, which, pz, py_half, count):
-        for i in range(count):
-            py = py_half * 4 + (y + 1 + i) % 4
+    others = []
+    for k in range(8):
+        py = (y + far_first(k, 4)) % 8
+        others.append((py // 2, x * 4 + (py % 2) * 2 + core, py // 4, pl.multiple_of((py % 4) * 8, 8)))
+
+    def send_tiles(src, skip, got, which, pz, count=8):
+        for py_hi, pdomain, half, row in others[:count]:
             rdma(
-                src.at[skip + pz * 2 + py_half, pl.ds(pl.multiple_of((py % 4) * 8, 8), 8)], got.at[zy],
-                a2a_send.at[which], a2a_recv.at[which], at(pz, py, x, core),
+                src.at[skip + pz * 2 + half, pl.ds(row, 8)], got.at[zy],
+                a2a_send.at[which], a2a_recv.at[which], (pz * 4 + py_hi, pdomain),
             ).start()
 
     def keep_tile(src, skip, got):
-        got[zy] = src[skip + zy // 4, pl.ds(pl.multiple_of((zy % 4) * 8, 8), 8)]
+        got[zy] = src[skip + zy // 4, pl.ds(others[7][3], 8)]
 
     def all_tiles(got, which):
         return rdma(got.at[pl.ds(0, 63)], got.at[pl.ds(0, 63)], a2a_send.at[which], a2a_recv.at[which], mate)
 
-    def filtered_out(j, _):
-        pz, half = turn(j)
-        send_tiles(fil, 6, gf, 0, pz, half, 4)
+    def filtered_out(i, _):
+        send_tiles(fil, 6, gf, 0, (z + far_first(i, 4)) % 8)
+        for j in (2 * i, 2 * i + 1):
+            acc[j] = part_y(fil[j + 6])
+        return 0
+
+    lax.fori_loop(0, 7, filtered_out, 0)
+    send_tiles(fil, 6, gf, 0, z, 7)
+    keep_tile(fil, 6, gf)
+    for j in (14, 15):
         acc[j] = part_y(fil[j + 6])
-        return 0
-
-    lax.fori_loop(0, CX - 1, filtered_out, 0)
-    send_tiles(fil, 6, gf, 0, z, y // 4, 3)
-    keep_tile(fil, 6, gf)
-    acc[CX - 1] = part_y(fil[CX + 5])
     hear(5)
     tell(6)
 
@@ -272,49 +274,54 @@
     for c in rims[4:]:
         c.wait_recv()
 
-    def applied_layer(k):
-        hf[k] = acc[k] + part_x(fil, k + 6) + pot[k] * fil[k + 6]
-
-    def applied_out(j, _):
-        pz, half = turn(j)
-        applied_layer(pz * 2 + half)
-        send_tiles(hf, 0, gh, 1, pz, half, 4)
+    def applied_layers(pz):
+        for k in (2 * pz, 2 * pz + 1):
+            hf[k] = acc[k] + part_x(fil, k + 6) + pot[k] * fil[k + 6]
+
+    def applied_out(i, _):
+        pz = (z + far_first(i, 4)) % 8
+        applied_layers(pz)
+        send_tiles(hf, 0, gh, 1, pz)
         return 0
 
-    lax.fori_loop(0, CX - 1, applied_out, 0)
-    applied_layer(zy // 4)
-    send_tiles(hf, 0, gh, 1, z, y // 4, 3)
+    lax.fori_loop(0, 7, applied_out, 0)
+    applied_layers(z)
+    send_tiles(hf, 0, gh, 1, z, 7)
     keep_tile(hf, 0, gh)
 
     def contract(left, right):
-        return lax.dot_general(
-            left, right, (((1,), (1,)), ((), ())),
-            precision=lax.Precision.HIGHEST, preferred_element_type=jnp.float32,
-        )
+        return lax.dot_general(left, right, (((1,), (1,)), ((), ())), preferred_element_type=jnp.float32)
+
+    def halves(value):
+        upper = value.astype(jnp.bfloat16)
+        return upper, (value - upper.astype(jnp.float32)).astype(jnp.bfloat16)
+
+    def cells(got, s):
+        return jnp.concatenate([got[:, 2 * s, :], got[:, 2 * s + 1, :]], axis=1)
 
     hear(7)
     all_tiles(gf, 0).wait_recv()
     over = jnp.zeros((NB, NB), jnp.float32)
-    for s in range(8):
-        over = over + contract(gf[:, s, :], gf[:, s, :])
+    for s in range(4):
+        upper, lower = halves(cells(gf, s))
+        g_high[s] = upper
+        g_low[s] = lower
+        over = over + (contract(upper, upper) + (contract(upper, lower) + contract(lower, upper)))
     part[:, :, :NB] = over.reshape(8, 8, NB)
     all_tiles(gh, 1).wait_recv()
     proj = jnp.zeros((NB, NB), jnp.float32)
-    for s in range(8):
-        proj = proj + contract(gf[:, s, :], gh[:, s, :])
+    for s in range(4):
+        upper, lower = halves(cells(gh, s))
+        proj = proj + (contract(g_high[s], upper) + (contract(g_high[s], lower) + contract(g_low[s], upper)))
     part[:, :, NB:] = proj.reshape(8, 8, NB)
 
     slot = z * 2 + yl
 
-    def send_rows(j, _):
-        pz, py = (z + far_first(j // 2, 4)) % 8, (yl + 1 + j) % 2
-        rdma(
-            part.at[pz], r1.at[slot], red_send.at[0], red_recv.at[0],
-            (pz * 4 + yh, x * 4 + py * 2 + core),
-        ).start()
-        return 0
-
-    lax.fori_loop(0, 15, send_rows, 0)
+    sides = [x * 4 + (1 - yl) * 2 + core, domain]
+    for i in range(8):
+        pz = (z + far_first(i, 4)) % 8
+        for to in sides[: 2 if i < 7 else 1]:
+            rdma(part.at[pz], r1.at[slot], red_send.at[0], red_recv.at[0], (pz * 4 + yh, to)).start()
     back = rdma(fil.at[mid, rows_other], out_f.at[yl], back_send, back_recv, at(z, yo, x, core))
     back.start()
     keep = pltpu.make_async_copy(fil.at[mid, rows], out_f.at[yl], loc_sem.at[2])
@@ -328,19 +335,19 @@
         tot[i] = total[2 * i : 2 * i + 2]
     slot2 = yh * 8 + x * 2 + core
 
-    def send_total(j, _):
-        ph, px = (yh + far_first(j // 8, 2)) % 4, (x + far_first((j // 2) % 4, 2)) % 4
-        rdma(
-            tot.at[ph], r2.at[slot2], red_send.at[1], red_recv.at[1],
-            (z * 4 + ph, px * 4 + yl * 2 + (core + 1 + j) % 2),
-        ).start()
-        return 0
-
-    lax.fori_loop(0, 31, send_total, 0)
+    columns = [
+        ((x + far_first(i, 2)) % 4) * 4 + yl * 2 + c for i in range(4) for c in (1 - core, core)
+    ]
+    for i in range(4):
+        ph = (yh + far_first(i, 2)) % 4
+        for to in columns[: 8 if i < 3 else 7]:
+            rdma(tot.at[ph], r2.at[slot2], red_send.at[1], red_recv.at[1], (z * 4 + ph, to)).start()
     r2[slot2] = tot[yh]
     red2 = rdma(r2.at[pl.ds(0, 31)], r2.at[pl.ds(0, 31)], red_send.at[1], red_recv.at[1], mate)
     red2.wait_recv()
-    out_sp[...] = jnp.sum(r2[...], axis=0) * (1.0 / NCELL)
+    result = jnp.sum(r2[...], axis=0) * (1.0 / NCELL)
+    out_s[...] = result[:, :NB]
+    out_p[...] = result[:, NB:]
 
     for c in swaps + direct + [given]:
         c.wait_send()
@@ -356,28 +363,33 @@
     back.wait()
 
 
-def deliver(filtered, both, out_f, out_s, out_p, sem):
-    whole = pltpu.make_async_copy(filtered, out_f, sem)
-    whole.start()
-    out_s[...] = both[:, :NB]
-    out_p[...] = both[:, NB:]
-    whole.wait()
+def deliver(filtered, inter, proj, out_f, out_s, out_p, sem):
+    copies = [
+        pltpu.make_async_copy(src, dst, sem.at[i])
+        for i, (src, dst) in enumerate(((filtered, out_f), (inter, out_s), (proj, out_p)))
+    ]
+    for c in copies:
+        c.start()
+    for c in copies:
+        c.wait()
 
 
 def shards(orbitals, potential):
     f32 = jnp.float32
     vmem = pltpu.VMEM
     dma = pltpu.SemaphoreType.DMA
+    any_ = pl.BlockSpec(memory_space=pl.ANY)
     hbm = pl.BlockSpec(memory_space=pltpu.HBM)
     full = pl.BlockSpec(memory_space=pltpu.VMEM)
-    filtered, both = pl.pallas_call(
+    filtered, inter, proj = pl.pallas_call(
         kernel,
         out_shape=(
             jax.ShapeDtypeStruct((2, CX, CY, CZ), f32),
-            jax.ShapeDtypeStruct((2, 2 * NB), f32),
+            jax.ShapeDtypeStruct((2, NB), f32),
+            jax.ShapeDtypeStruct((2, NB), f32),
         ),
         in_specs=[hbm, hbm],
-        out_specs=(hbm, full),
+        out_specs=(hbm, full, full),
         scratch_shapes=[
             vmem((CX + 12, NY, CZ), f32),
             vmem((CX, NY, CZ), f32),
@@ -390,6 +402,8 @@
             vmem((CX, NY, CZ), f32),
             vmem((NB, 8, CZ), f32),
             vmem((NB, 8, CZ), f32),
+            vmem((4, NB, 2 * CZ), jnp.bfloat16),
+            vmem((4, NB, 2 * CZ), jnp.bfloat16),
             vmem((8, 8, 2 * NB), f32),
             vmem((16, 8, 2 * NB), f32),
             vmem((32, 2, 2 * NB), f32),
@@ -413,12 +427,12 @@
             jax.ShapeDtypeStruct((2, NB), f32),
             jax.ShapeDtypeStruct((2, NB), f32),
         ),
-        in_specs=[pl.BlockSpec(memory_space=pl.ANY), full],
-        out_specs=(hbm, full, full),
-        scratch_shapes=[dma],
+        in_specs=[any_, any_, any_],
+        out_specs=(hbm, hbm, hbm),
+        scratch_shapes=[dma((3,))],
         compiler_params=pltpu.CompilerParams(vmem_limit_bytes=32 << 20),
         name="deliver",
-    )(filtered, both)
+    )(filtered, inter, proj)
     return filtered[:, None], inter, proj
 
 

time: 55.8 us -> 54.2 us (0.971)
  Pallas kernels: 55 us -> 53.4 us
    pallas_call x1, Pallas kernels: 53.7 us -> 52.7 us  [shards(): pl.pallas_call(kernel, out_shape=(jax.ShapeDtypeStruct((2, CX, CY, CZ), f...]
where the time goes in v5:
time: 54.2 us; the launch traced here: 54.1 us
  Pallas kernels  53.4 us (99%)
  between operations  0.64 us (1%)
    pallas_call x1, Pallas kernels, shards(): pl.pallas_call(kernel, out_shape=(jax.ShapeDtypeStruct((2, CX, CY, CZ), f...  52.7 us

profile of v5, /device:TPU:1, one launch (start us, length us, event | category | flops | bytes accessed | tf_op | source)
XLA Modules:
  0.0 54.1 jit_solution(13771958317852675422)
XLA Ops:
  0.6 52.7 %chebyshev_step.1 = (f32[2,16,16,128]{3,2,1,0:T(8,128)S(1)}, f32[2,64]{1,0:T(2,128)S(1)}, f32[2,64]{1,0:T(2,128)S(1)}) custom-call(f32[2,16,16,128]{3,2,1,0:T(8,128)} %bitcast.5, f32[16,16,128]{2,1,0:T(8,128)} %bitcast.6), custom_call_target="tpu_custom_call" | custom-call | tf_op jit(solution)/shard_map/chebyshev_step/pallas_call | solution.py:384
  53.3 0.7 %deliver.1 = (f32[2,16,16,128]{3,2,1,0:T(8,128)}, f32[2,64]{1,0:T(2,128)}, f32[2,64]{1,0:T(2,128)}) custom-call(f32[2,16,16,128]{3,2,1,0:T(8,128)S(1)} %get-tuple-element.9.filtered, f32[2,64]{1,0:T(2,128)S(1)} %get-tuple-element.10.inter, f32[2,64]{1,0:T(2,128)S(1)} %get-tuple-element.11.proj), custom_call_target="tpu_custom_call" | custom-call | tf_op jit(solution)/shard_map/deliver/pallas_call | solution.py:423

commit v6 on v5

--- a/solution.py
+++ b/solution.py
@@ -59,7 +59,7 @@
 
 def kernel(
     orb_in, pot_in, out_f, out_s, out_p,
-    orb, pot, first, fil, zo, zf, zs, acc, hf, gf, gh, g_high, g_low, part, r1, r2, tot,
+    orb, give, pot, first, fil, zo, zf, zs, acc, hf, gf, gh, g_high, g_low, part, r1, r2, both_cores, tot,
     loc_sem, in_send, in_recv, core_send, core_recv, x_send, x_recv,
     a2a_send, a2a_recv, back_send, back_recv, red_send, red_recv, ring,
 ):
@@ -94,6 +94,7 @@
 
     local = [
         pltpu.make_async_copy(orb_in.at[yl], orb.at[mid, rows], loc_sem.at[0]),
+        pltpu.make_async_copy(orb_in.at[1 - yl], give, loc_sem.at[3]),
         pltpu.make_async_copy(pot_in, pot.at[:, rows], loc_sem.at[1]),
     ]
     for c in local:
@@ -105,6 +106,8 @@
     for to in (up_y, down_y, to_xn, to_xp, up_z, down_z, mate):
         pl.semaphore_signal(bar, inc=1, device_id=to, device_id_type=MESH)
     pl.semaphore_wait(bar, 7)
+    for c in local:
+        c.wait()
 
     far_z = (at((z + 2) % 8, y, x, core), at((z + 6) % 8, y, x, core))
     far_y = (at(z, (y + 2) % 8, x, core), at(z, (y + 6) % 8, x, core))
@@ -121,28 +124,26 @@
 
     swaps = [
         rdma(
-            orb_in.at[1 - yl, pl.ds(k, n)], orb.at[pl.ds(k + 6, n), rows],
+            give.at[pl.ds(k, n)], orb.at[pl.ds(k + 6, n), rows],
             in_send.at[i], in_recv.at[i], at(z, yo, x, core),
         )
         for i, (k, n) in enumerate(((0, 6), (10, 6), (6, 4)))
     ]
     direct = [
-        rdma(orb_in.at[yl, pl.ds(10, 6)], orb.at[low, rows], in_send.at[3], in_recv.at[3], to_xn),
-        rdma(orb_in.at[yl, pl.ds(0, 6)], orb.at[high, rows], in_send.at[4], in_recv.at[4], to_xp),
+        rdma(orb.at[pl.ds(16, 6), rows], orb.at[low, rows], in_send.at[3], in_recv.at[3], to_xn),
+        rdma(orb.at[pl.ds(6, 6), rows], orb.at[high, rows], in_send.at[4], in_recv.at[4], to_xp),
     ]
-    given = rdma(pot_in, pot.at[:, rows], in_send.at[5], in_recv.at[5], at(z, yq, x, core))
+    given = rdma(pot.at[:, rows], pot.at[:, rows], in_send.at[5], in_recv.at[5], at(z, yq, x, core))
 
     def to_mate(k, src, dst):
         c = rdma(src, dst, core_send.at[k], core_recv.at[k], mate)
         c.start()
         return c
 
-    beside = [to_mate(0, orb_in.at[yl], zo.at[:, rows])]
     for c in swaps[:2] + direct + [given]:
         c.start()
+    beside = [to_mate(0, orb.at[mid, rows], zo.at[:, rows])]
     tell(0)
-    for c in local:
-        c.wait()
 
     lane = lax.broadcasted_iota(jnp.int32, (NY, CZ), 1)
     lane_half = lax.broadcasted_iota(jnp.int32, (CY, CZ), 1)
@@ -197,15 +198,15 @@
     beside[1].wait_recv()
     over_layers(along_z_half(rows_other))
     given.wait_recv()
-    for c in direct + rims:
-        c.wait_recv()
-
-    def by_edges(body, src, k):
+
+    def inner(body):
+        over_layers(body, 6, 4)
+
+    def edges(body, src, k):
         over_layers(body, 0, 6)
         sent = [rim(src, k, False)]
         over_layers(body, 10, 6)
         sent.append(rim(src, k + 1, True))
-        over_layers(body, 6, 4)
         beside.append(to_mate(k // 2 + 1, src.at[mid], zf if k == 2 else zs))
         return sent
 
@@ -214,7 +215,10 @@
         h = acc[k] + hf[k] + part_x(orb, k + 6) + (pot[k] - filter_center) * here
         first[k + 6] = h * (1.0 / filter_half)
 
-    rims += by_edges(last_first, first, 2)
+    inner(last_first)
+    for c in direct + rims:
+        c.wait_recv()
+    rims += edges(last_first, first, 2)
 
     hear(2)
     tell(3)
@@ -225,68 +229,89 @@
     over_layers(along_z(first, zf))
     hear(4)
     tell(5)
-    for c in rims[2:]:
-        c.wait_recv()
+
+    def layer_of(group, pz):
+        m = pz // 2
+        return (6 + m, m, 4 + m + 4 * (m // 2), 12 + m)[group]
+
+    def send_tiles(src, skip, got, which, pz, groups, at_home=False):
+        for group in groups:
+            for b in range(2):
+                py = (pz + group + 4 * b) % 8
+                row = pl.multiple_of(16 * b + 8 * (pz % 2), 8)
+                copy = rdma(
+                    src.at[skip + layer_of(group, pz), pl.ds(row, 8)], got.at[zy],
+                    a2a_send.at[which], a2a_recv.at[which], at(pz, py, x, core),
+                )
+                if at_home:
+                    pl.when(py != y)(copy.start)
+                else:
+                    copy.start()
+
+    def all_tiles(got, which):
+        return rdma(got.at[pl.ds(0, 63)], got.at[pl.ds(0, 63)], a2a_send.at[which], a2a_recv.at[which], mate)
+
+    def send_inner(src, skip, got, which):
+        def turn(i, _):
+            send_tiles(src, skip, got, which, (z + far_first(i, 4)) % 8, (0,))
+            return 0
+
+        lax.fori_loop(0, 7, turn, 0)
+        send_tiles(src, skip, got, which, z, (0,), True)
+
+    def keep_tile(src, skip, got):
+        group, b = (y + 8 - z) % 4, ((y + 8 - z) % 8) // 4
+        row = pl.multiple_of(16 * b + 8 * (z % 2), 8)
+        for k in range(4):
+            @pl.when(group == k)
+            def _():
+                got[zy] = src[skip + layer_of(k, z), pl.ds(row, 8)]
 
     def last_filtered(k):
         here = first[k + 6]
         h = acc[k] + part_x(first, k + 6) + (pot[k] - filter_center) * here
         fil[k + 6] = h * (2.0 / filter_half) - orb[k + 6]
 
-    rims += by_edges(last_filtered, fil, 4)
-
-    others = []
-    for k in range(8):
-        py = (y + far_first(k, 4)) % 8
-        others.append((py // 2, x * 4 + (py % 2) * 2 + core, py // 4, pl.multiple_of((py % 4) * 8, 8)))
-
-    def send_tiles(src, skip, got, which, pz, count=8):
-        for py_hi, pdomain, half, row in others[:count]:
-            rdma(
-                src.at[skip + pz * 2 + half, pl.ds(row, 8)], got.at[zy],
-                a2a_send.at[which], a2a_recv.at[which], (pz * 4 + py_hi, pdomain),
-            ).start()
-
-    def keep_tile(src, skip, got):
-        got[zy] = src[skip + zy // 4, pl.ds(others[7][3], 8)]
-
-    def all_tiles(got, which):
-        return rdma(got.at[pl.ds(0, 63)], got.at[pl.ds(0, 63)], a2a_send.at[which], a2a_recv.at[which], mate)
+    inner(last_filtered)
+    send_inner(fil, 6, gf, 0)
+    for c in rims[2:4]:
+        c.wait_recv()
+    rims += edges(last_filtered, fil, 4)
 
     def filtered_out(i, _):
-        send_tiles(fil, 6, gf, 0, (z + far_first(i, 4)) % 8)
+        send_tiles(fil, 6, gf, 0, (z + far_first(i, 4)) % 8, (1, 2, 3))
         for j in (2 * i, 2 * i + 1):
             acc[j] = part_y(fil[j + 6])
         return 0
 
     lax.fori_loop(0, 7, filtered_out, 0)
-    send_tiles(fil, 6, gf, 0, z, 7)
+    send_tiles(fil, 6, gf, 0, z, (1, 2, 3), True)
     keep_tile(fil, 6, gf)
     for j in (14, 15):
         acc[j] = part_y(fil[j + 6])
     hear(5)
     tell(6)
 
+    def applied_layer(k):
+        hf[k] = acc[k] + part_x(fil, k + 6) + pot[k] * fil[k + 6]
+
     beside[3].wait_recv()
     over_layers(along_z(fil, zs))
     hear(6)
     tell(7)
+    inner(applied_layer)
+    send_inner(hf, 0, gh, 1)
     for c in rims[4:]:
         c.wait_recv()
-
-    def applied_layers(pz):
-        for k in (2 * pz, 2 * pz + 1):
-            hf[k] = acc[k] + part_x(fil, k + 6) + pot[k] * fil[k + 6]
+    over_layers(applied_layer, 0, 6)
+    over_layers(applied_layer, 10, 6)
 
     def applied_out(i, _):
-        pz = (z + far_first(i, 4)) % 8
-        applied_layers(pz)
-        send_tiles(hf, 0, gh, 1, pz)
+        send_tiles(hf, 0, gh, 1, (z + far_first(i, 4)) % 8, (1, 2, 3))
         return 0
 
     lax.fori_loop(0, 7, applied_out, 0)
-    applied_layers(z)
-    send_tiles(hf, 0, gh, 1, z, 7)
+    send_tiles(hf, 0, gh, 1, z, (1, 2, 3), True)
     keep_tile(hf, 0, gh)
 
     def contract(left, right):
@@ -330,20 +355,21 @@
     red1 = rdma(r1.at[pl.ds(0, 15)], r1.at[pl.ds(0, 15)], red_send.at[0], red_recv.at[0], mate)
     red1.wait_recv()
 
-    total = jnp.sum(r1[...], axis=0)
+    both_cores[0] = jnp.sum(r1[...], axis=0)
+    red3 = rdma(both_cores.at[0], both_cores.at[1], red_send.at[2], red_recv.at[2], mate)
+    red3.start()
+    red3.wait_recv()
+    total = both_cores[0] + both_cores[1]
     for i in range(4):
         tot[i] = total[2 * i : 2 * i + 2]
-    slot2 = yh * 8 + x * 2 + core
-
-    columns = [
-        ((x + far_first(i, 2)) % 4) * 4 + yl * 2 + c for i in range(4) for c in (1 - core, core)
-    ]
+    slot2 = yh * 4 + x
+    columns = [((x + far_first(i, 2)) % 4) * 4 + yl * 2 + core for i in range(4)]
     for i in range(4):
         ph = (yh + far_first(i, 2)) % 4
-        for to in columns[: 8 if i < 3 else 7]:
+        for to in columns[: 4 if i < 3 else 3]:
             rdma(tot.at[ph], r2.at[slot2], red_send.at[1], red_recv.at[1], (z * 4 + ph, to)).start()
     r2[slot2] = tot[yh]
-    red2 = rdma(r2.at[pl.ds(0, 31)], r2.at[pl.ds(0, 31)], red_send.at[1], red_recv.at[1], mate)
+    red2 = rdma(r2.at[pl.ds(0, 15)], r2.at[pl.ds(0, 15)], red_send.at[1], red_recv.at[1], mate)
     red2.wait_recv()
     result = jnp.sum(r2[...], axis=0) * (1.0 / NCELL)
     out_s[...] = result[:, :NB]
@@ -359,6 +385,7 @@
     all_tiles(gh, 1).wait_send()
     red1.wait_send()
     red2.wait_send()
+    red3.wait_send()
     keep.wait()
     back.wait()
 
@@ -392,6 +419,7 @@
         out_specs=(hbm, full, full),
         scratch_shapes=[
             vmem((CX + 12, NY, CZ), f32),
+            vmem((CX, CY, CZ), f32),
             vmem((CX, NY, CZ), f32),
             vmem((CX + 12, NY, CZ), f32),
             vmem((CX + 12, NY, CZ), f32),
@@ -406,10 +434,11 @@
             vmem((4, NB, 2 * CZ), jnp.bfloat16),
             vmem((8, 8, 2 * NB), f32),
             vmem((16, 8, 2 * NB), f32),
-            vmem((32, 2, 2 * NB), f32),
+            vmem((16, 2, 2 * NB), f32),
+            vmem((2, 8, 2 * NB), f32),
             vmem((4, 2, 2 * NB), f32),
-            dma((3,)), dma((6,)), dma((6,)), dma((4,)), dma((4,)), dma((6,)), dma((6,)),
-            dma((2,)), dma((2,)), dma, dma, dma((2,)), dma((2,)),
+            dma((4,)), dma((6,)), dma((6,)), dma((4,)), dma((4,)), dma((6,)), dma((6,)),
+            dma((2,)), dma((2,)), dma, dma, dma((3,)), dma((3,)),
             pltpu.SemaphoreType.REGULAR((8,)),
         ],
         compiler_params=pltpu.CompilerParams(

time: 54.2 us -> 55.2 us (1.018)
  Pallas kernels: 53.4 us -> 54.5 us
    pallas_call x1, Pallas kernels: 52.7 us -> 53.7 us  [shards(): pl.pallas_call(kernel, out_shape=(jax.ShapeDtypeStruct((2, CX, CY, CZ), f...]
where the time goes in v6:
time: 55.2 us; the launch traced here: 55.1 us
  Pallas kernels  54.5 us (99%)
  between operations  0.64 us (1%)
    pallas_call x1, Pallas kernels, shards(): pl.pallas_call(kernel, out_shape=(jax.ShapeDtypeStruct((2, CX, CY, CZ), f...  53.7 us

profile of v6, /device:TPU:1, one launch (start us, length us, event | category | flops | bytes accessed | tf_op | source)
XLA Modules:
  0.0 55.1 jit_solution(17786581107094502969)
XLA Ops:
  0.6 53.7 %chebyshev_step.1 = (f32[2,16,16,128]{3,2,1,0:T(8,128)S(1)}, f32[2,64]{1,0:T(2,128)S(1)}, f32[2,64]{1,0:T(2,128)S(1)}) custom-call(f32[2,16,16,128]{3,2,1,0:T(8,128)} %bitcast.5, f32[16,16,128]{2,1,0:T(8,128)} %bitcast.6), custom_call_target="tpu_custom_call" | custom-call | tf_op jit(solution)/shard_map/chebyshev_step/pallas_call | solution.py:411
  54.4 0.7 %deliver.1 = (f32[2,16,16,128]{3,2,1,0:T(8,128)}, f32[2,64]{1,0:T(2,128)}, f32[2,64]{1,0:T(2,128)}) custom-call(f32[2,16,16,128]{3,2,1,0:T(8,128)S(1)} %get-tuple-element.9.filtered, f32[2,64]{1,0:T(2,128)S(1)} %get-tuple-element.10.inter, f32[2,64]{1,0:T(2,128)S(1)} %get-tuple-element.11.proj), custom_call_target="tpu_custom_call" | custom-call | tf_op jit(solution)/shard_map/deliver/pallas_call | solution.py:452

commit v7 on v6

--- a/solution.py
+++ b/solution.py
@@ -59,7 +59,7 @@
 
 def kernel(
     orb_in, pot_in, out_f, out_s, out_p,
-    orb, give, pot, first, fil, zo, zf, zs, acc, hf, gf, gh, g_high, g_low, part, r1, r2, both_cores, tot,
+    orb, give, pot, first, fil, zo, zf, zs, acc, along, hf, gf, gh, g_high, g_low, part, r1, r2, tot,
     loc_sem, in_send, in_recv, core_send, core_recv, x_send, x_recv,
     a2a_send, a2a_recv, back_send, back_recv, red_send, red_recv, ring,
 ):
@@ -93,9 +93,9 @@
     rows_other = pl.ds(other, CY)
 
     local = [
-        pltpu.make_async_copy(orb_in.at[yl], orb.at[mid, rows], loc_sem.at[0]),
+        pltpu.make_async_copy(orb_in.at[yl], orb.at[pl.ds(12, CX), rows], loc_sem.at[0]),
         pltpu.make_async_copy(orb_in.at[1 - yl], give, loc_sem.at[3]),
-        pltpu.make_async_copy(pot_in, pot.at[:, rows], loc_sem.at[1]),
+        pltpu.make_async_copy(pot_in, pot.at[mid, rows], loc_sem.at[1]),
     ]
     for c in local:
         c.start()
@@ -103,9 +103,10 @@
     bar = pltpu.get_barrier_semaphore()
     up_z, down_z = at((z + 1) % 8, y, x, core), at((z + 7) % 8, y, x, core)
     up_y, down_y = at(z, (y + 1) % 8, x, core), at(z, (y + 7) % 8, x, core)
-    for to in (up_y, down_y, to_xn, to_xp, up_z, down_z, mate):
+    across = [at(z, yq, xn, core), at(z, yq, xp, core)]
+    for to in (up_y, down_y, to_xn, to_xp, up_z, down_z, mate, *across):
         pl.semaphore_signal(bar, inc=1, device_id=to, device_id_type=MESH)
-    pl.semaphore_wait(bar, 7)
+    pl.semaphore_wait(bar, 9)
     for c in local:
         c.wait()
 
@@ -122,27 +123,33 @@
     def hear(k):
         pl.semaphore_wait(ring.at[k], len(words[k]))
 
+    def entry(k, src, dst, to):
+        return rdma(src, dst, in_send.at[k], in_recv.at[k], to)
+
     swaps = [
-        rdma(
-            give.at[pl.ds(k, n)], orb.at[pl.ds(k + 6, n), rows],
-            in_send.at[i], in_recv.at[i], at(z, yo, x, core),
-        )
-        for i, (k, n) in enumerate(((0, 6), (10, 6), (6, 4)))
+        entry(0, give.at[pl.ds(0, 8)], orb.at[pl.ds(12, 8), rows], at(z, yo, x, core)),
+        entry(1, give.at[pl.ds(8, 8)], orb.at[pl.ds(20, 8), rows], at(z, yo, x, core)),
     ]
     direct = [
-        rdma(orb.at[pl.ds(16, 6), rows], orb.at[low, rows], in_send.at[3], in_recv.at[3], to_xn),
-        rdma(orb.at[pl.ds(6, 6), rows], orb.at[high, rows], in_send.at[4], in_recv.at[4], to_xp),
+        entry(2, orb.at[pl.ds(16, 12), rows], orb.at[pl.ds(0, 12), rows], to_xn),
+        entry(3, orb.at[pl.ds(12, 12), rows], orb.at[pl.ds(28, 12), rows], to_xp),
     ]
-    given = rdma(pot.at[:, rows], pot.at[:, rows], in_send.at[5], in_recv.at[5], at(z, yq, x, core))
+    given = [
+        entry(4, pot.at[mid, rows], pot.at[mid, rows], at(z, yq, x, core)),
+        entry(5, pot.at[pl.ds(16, 6), rows], pot.at[low, rows], to_xn),
+        entry(6, pot.at[pl.ds(6, 6), rows], pot.at[high, rows], to_xp),
+        entry(7, pot.at[pl.ds(16, 6), rows], pot.at[low, rows], across[0]),
+        entry(8, pot.at[pl.ds(6, 6), rows], pot.at[high, rows], across[1]),
+    ]
 
     def to_mate(k, src, dst):
         c = rdma(src, dst, core_send.at[k], core_recv.at[k], mate)
         c.start()
         return c
 
-    for c in swaps[:2] + direct + [given]:
-        c.start()
-    beside = [to_mate(0, orb.at[mid, rows], zo.at[:, rows])]
+    for c in swaps + direct + given:
+        c.start()
+    beside = [to_mate(0, orb.at[pl.ds(12, CX), rows], zo.at[mid, rows])]
     tell(0)
 
     lane = lax.broadcasted_iota(jnp.int32, (NY, CZ), 1)
@@ -155,6 +162,23 @@
 
         lax.fori_loop(first_layer, first_layer + count, step, 0)
 
+    def halo_layers(body):
+        over_layers(body, 0, 6)
+        over_layers(body, 22, 6)
+
+    def orb_along_y(k):
+        acc[k] = part_y(orb[k + 6])
+
+    def orb_along_z(at_rows):
+        def body(k):
+            along[k, at_rows] = part_z(orb[k + 6, at_rows], zo[k, at_rows], lane_half)
+
+        return body
+
+    def orb_along_x(k):
+        h = acc[k] + along[k] + part_x(orb, k + 6) + (pot[k] - filter_center) * orb[k + 6]
+        first[k] = h * (1.0 / filter_half)
+
     def along_y(src):
         def body(k):
             acc[k] = part_y(src[k + 6])
@@ -167,68 +191,78 @@
 
         return body
 
-    def along_z_half(at_rows):
-        def body(k):
-            hf[k, at_rows] = part_z(orb[k + 6, at_rows], zo[k, at_rows], lane_half)
-
-        return body
-
-    def rim(src, k, to_next, at_rows=slice(None)):
-        if to_next:
-            c = rdma(src.at[pl.ds(16, 6), at_rows], src.at[low, at_rows], x_send.at[k], x_recv.at[k], to_xn)
-        else:
-            c = rdma(src.at[pl.ds(6, 6), at_rows], src.at[high, at_rows], x_send.at[k], x_recv.at[k], to_xp)
+    def forward(k, start, count, to, dst):
+        c = rdma(
+            orb.at[pl.ds(start, count), rows_other], orb.at[pl.ds(dst, count), rows_other],
+            x_send.at[k], x_recv.at[k], to,
+        )
         c.start()
         return c
 
-    swaps[2].start()
     beside[0].wait_recv()
-    over_layers(along_z_half(rows))
+    over_layers(orb_along_z(rows), 6)
     hear(0)
     tell(1)
     swaps[0].wait_recv()
-    rims = [rim(orb, 0, False, rows_other)]
+    rims = [forward(0, 12, 8, to_xp, 28), forward(1, 16, 4, to_xn, 0)]
     swaps[1].wait_recv()
-    rims.append(rim(orb, 1, True, rows_other))
-    swaps[2].wait_recv()
-    beside.append(to_mate(1, orb.at[mid, rows_other], zo.at[:, rows_other]))
-    over_layers(along_y(orb))
+    rims += [forward(2, 20, 4, to_xp, 36), forward(3, 20, 8, to_xn, 4)]
+    beside.append(to_mate(1, orb.at[pl.ds(12, CX), rows_other], zo.at[mid, rows_other]))
+    for c in direct:
+        c.wait_recv()
+    beside.append(to_mate(2, orb.at[pl.ds(6, 6), rows], zo.at[low, rows]))
+    beside.append(to_mate(3, orb.at[pl.ds(28, 6), rows], zo.at[high, rows]))
+    over_layers(orb_along_y, 6)
     hear(1)
     tell(2)
     beside[1].wait_recv()
-    over_layers(along_z_half(rows_other))
-    given.wait_recv()
-
-    def inner(body):
-        over_layers(body, 6, 4)
-
-    def edges(body, src, k):
-        over_layers(body, 0, 6)
-        sent = [rim(src, k, False)]
-        over_layers(body, 10, 6)
-        sent.append(rim(src, k + 1, True))
-        beside.append(to_mate(k // 2 + 1, src.at[mid], zf if k == 2 else zs))
-        return sent
-
-    def last_first(k):
-        here = orb[k + 6]
-        h = acc[k] + hf[k] + part_x(orb, k + 6) + (pot[k] - filter_center) * here
-        first[k + 6] = h * (1.0 / filter_half)
-
-    inner(last_first)
-    for c in direct + rims:
+    over_layers(orb_along_z(rows_other), 6)
+    beside[2].wait_recv()
+    beside[3].wait_recv()
+    halo_layers(orb_along_z(rows))
+    given[0].wait_recv()
+    over_layers(orb_along_x, 12, 4)
+    for c in rims:
         c.wait_recv()
-    rims += edges(last_first, first, 2)
-
+    beside.append(to_mate(4, orb.at[pl.ds(6, 6), rows_other], zo.at[low, rows_other]))
+    beside.append(to_mate(5, orb.at[pl.ds(28, 6), rows_other], zo.at[high, rows_other]))
+    over_layers(orb_along_x, 6, 6)
+    over_layers(orb_along_x, 16, 6)
+    beside.append(to_mate(6, first.at[mid], zf))
+    halo_layers(orb_along_y)
     hear(2)
     tell(3)
+    for c in given[1:]:
+        c.wait_recv()
+    beside[4].wait_recv()
+    beside[5].wait_recv()
+    halo_layers(orb_along_z(rows_other))
+    halo_layers(orb_along_x)
+
     over_layers(along_y(first))
     hear(3)
     tell(4)
-    beside[2].wait_recv()
+    beside[6].wait_recv()
     over_layers(along_z(first, zf))
     hear(4)
     tell(5)
+
+    def last_filtered(k):
+        here = first[k + 6]
+        h = acc[k] + part_x(first, k + 6) + (pot[k + 6] - filter_center) * here
+        fil[k + 6] = h * (2.0 / filter_half) - orb[k + 12]
+
+    def rim(k, start, dst, to):
+        c = rdma(fil.at[pl.ds(start, 6)], fil.at[dst], x_send.at[k], x_recv.at[k], to)
+        c.start()
+        return c
+
+    over_layers(last_filtered, 0, 6)
+    rims.append(rim(4, 6, high, to_xp))
+    over_layers(last_filtered, 10, 6)
+    rims.append(rim(5, 16, low, to_xn))
+    over_layers(last_filtered, 6, 4)
+    beside.append(to_mate(7, fil.at[mid], zs))
 
     def layer_of(group, pz):
         m = pz // 2
@@ -267,25 +301,14 @@
             def _():
                 got[zy] = src[skip + layer_of(k, z), pl.ds(row, 8)]
 
-    def last_filtered(k):
-        here = first[k + 6]
-        h = acc[k] + part_x(first, k + 6) + (pot[k] - filter_center) * here
-        fil[k + 6] = h * (2.0 / filter_half) - orb[k + 6]
-
-    inner(last_filtered)
-    send_inner(fil, 6, gf, 0)
-    for c in rims[2:4]:
-        c.wait_recv()
-    rims += edges(last_filtered, fil, 4)
-
     def filtered_out(i, _):
-        send_tiles(fil, 6, gf, 0, (z + far_first(i, 4)) % 8, (1, 2, 3))
+        send_tiles(fil, 6, gf, 0, (z + far_first(i, 4)) % 8, (0, 1, 2, 3))
         for j in (2 * i, 2 * i + 1):
             acc[j] = part_y(fil[j + 6])
         return 0
 
     lax.fori_loop(0, 7, filtered_out, 0)
-    send_tiles(fil, 6, gf, 0, z, (1, 2, 3), True)
+    send_tiles(fil, 6, gf, 0, z, (0, 1, 2, 3), True)
     keep_tile(fil, 6, gf)
     for j in (14, 15):
         acc[j] = part_y(fil[j + 6])
@@ -293,13 +316,13 @@
     tell(6)
 
     def applied_layer(k):
-        hf[k] = acc[k] + part_x(fil, k + 6) + pot[k] * fil[k + 6]
-
-    beside[3].wait_recv()
+        hf[k] = acc[k] + part_x(fil, k + 6) + pot[k + 6] * fil[k + 6]
+
+    beside[7].wait_recv()
     over_layers(along_z(fil, zs))
     hear(6)
     tell(7)
-    inner(applied_layer)
+    over_layers(applied_layer, 6, 4)
     send_inner(hf, 0, gh, 1)
     for c in rims[4:]:
         c.wait_recv()
@@ -332,50 +355,50 @@
         g_high[s] = upper
         g_low[s] = lower
         over = over + (contract(upper, upper) + (contract(upper, lower) + contract(lower, upper)))
-    part[:, :, :NB] = over.reshape(8, 8, NB)
+    part[:, :, :NB] = over.reshape(32, 2, NB)
     all_tiles(gh, 1).wait_recv()
     proj = jnp.zeros((NB, NB), jnp.float32)
     for s in range(4):
         upper, lower = halves(cells(gh, s))
         proj = proj + (contract(g_high[s], upper) + (contract(g_high[s], lower) + contract(g_low[s], upper)))
-    part[:, :, NB:] = proj.reshape(8, 8, NB)
-
-    slot = z * 2 + yl
-
-    sides = [x * 4 + (1 - yl) * 2 + core, domain]
-    for i in range(8):
-        pz = (z + far_first(i, 4)) % 8
-        for to in sides[: 2 if i < 7 else 1]:
-            rdma(part.at[pz], r1.at[slot], red_send.at[0], red_recv.at[0], (pz * 4 + yh, to)).start()
+    part[:, :, NB:] = proj.reshape(32, 2, NB)
+
+    def send_rows(pz, at_home=False):
+        for k in range(8):
+            py = (y + far_first(k, 4)) % 8
+            if not (at_home and k == 7):
+                rdma(
+                    part.at[pz * 4 + py // 2], r1.at[zy], red_send.at[0], red_recv.at[0], at(pz, py, x, core)
+                ).start()
+
+    def rows_out(i, _):
+        send_rows((z + far_first(i, 4)) % 8)
+        return 0
+
+    lax.fori_loop(0, 7, rows_out, 0)
+    send_rows(z, True)
+    r1[zy] = part[band]
+    red1 = rdma(r1.at[pl.ds(0, 63)], r1.at[pl.ds(0, 63)], red_send.at[0], red_recv.at[0], mate)
+    red1.wait_recv()
     back = rdma(fil.at[mid, rows_other], out_f.at[yl], back_send, back_recv, at(z, yo, x, core))
     back.start()
     keep = pltpu.make_async_copy(fil.at[mid, rows], out_f.at[yl], loc_sem.at[2])
     keep.start()
-    r1[slot] = part[z]
-    red1 = rdma(r1.at[pl.ds(0, 15)], r1.at[pl.ds(0, 15)], red_send.at[0], red_recv.at[0], mate)
-    red1.wait_recv()
-
-    both_cores[0] = jnp.sum(r1[...], axis=0)
-    red3 = rdma(both_cores.at[0], both_cores.at[1], red_send.at[2], red_recv.at[2], mate)
-    red3.start()
-    red3.wait_recv()
-    total = both_cores[0] + both_cores[1]
+
+    tot[...] = jnp.sum(r1[...], axis=0)
+    slot = x * 2 + core
     for i in range(4):
-        tot[i] = total[2 * i : 2 * i + 2]
-    slot2 = yh * 4 + x
-    columns = [((x + far_first(i, 2)) % 4) * 4 + yl * 2 + core for i in range(4)]
-    for i in range(4):
-        ph = (yh + far_first(i, 2)) % 4
-        for to in columns[: 4 if i < 3 else 3]:
-            rdma(tot.at[ph], r2.at[slot2], red_send.at[1], red_recv.at[1], (z * 4 + ph, to)).start()
-    r2[slot2] = tot[yh]
-    red2 = rdma(r2.at[pl.ds(0, 15)], r2.at[pl.ds(0, 15)], red_send.at[1], red_recv.at[1], mate)
+        for pc in (1 - core, core)[: 2 if i < 3 else 1]:
+            to = at(z, y, (x + far_first(i, 2)) % 4, pc)
+            rdma(tot, r2.at[slot], red_send.at[1], red_recv.at[1], to).start()
+    r2[slot] = tot[...]
+    red2 = rdma(r2.at[pl.ds(0, 7)], r2.at[pl.ds(0, 7)], red_send.at[1], red_recv.at[1], mate)
     red2.wait_recv()
     result = jnp.sum(r2[...], axis=0) * (1.0 / NCELL)
     out_s[...] = result[:, :NB]
     out_p[...] = result[:, NB:]
 
-    for c in swaps + direct + [given]:
+    for c in swaps + direct + given:
         c.wait_send()
     for c in beside:
         c.wait_send()
@@ -385,7 +408,6 @@
     all_tiles(gh, 1).wait_send()
     red1.wait_send()
     red2.wait_send()
-    red3.wait_send()
     keep.wait()
     back.wait()
 
@@ -418,27 +440,27 @@
         in_specs=[hbm, hbm],
         out_specs=(hbm, full, full),
         scratch_shapes=[
-            vmem((CX + 12, NY, CZ), f32),
+            vmem((CX + 24, NY, CZ), f32),
             vmem((CX, CY, CZ), f32),
-            vmem((CX, NY, CZ), f32),
+            vmem((CX + 12, NY, CZ), f32),
+            vmem((CX + 12, NY, CZ), f32),
             vmem((CX + 12, NY, CZ), f32),
             vmem((CX + 12, NY, CZ), f32),
             vmem((CX, NY, CZ), f32),
             vmem((CX, NY, CZ), f32),
-            vmem((CX, NY, CZ), f32),
-            vmem((CX, NY, CZ), f32),
+            vmem((CX + 12, NY, CZ), f32),
+            vmem((CX + 12, NY, CZ), f32),
             vmem((CX, NY, CZ), f32),
             vmem((NB, 8, CZ), f32),
             vmem((NB, 8, CZ), f32),
             vmem((4, NB, 2 * CZ), jnp.bfloat16),
             vmem((4, NB, 2 * CZ), jnp.bfloat16),
-            vmem((8, 8, 2 * NB), f32),
-            vmem((16, 8, 2 * NB), f32),
-            vmem((16, 2, 2 * NB), f32),
-            vmem((2, 8, 2 * NB), f32),
-            vmem((4, 2, 2 * NB), f32),
-            dma((4,)), dma((6,)), dma((6,)), dma((4,)), dma((4,)), dma((6,)), dma((6,)),
-            dma((2,)), dma((2,)), dma, dma, dma((3,)), dma((3,)),
+            vmem((32, 2, 2 * NB), f32),
+            vmem((64, 2, 2 * NB), f32),
+            vmem((8, 2, 2 * NB), f32),
+            vmem((2, 2 * NB), f32),
+            dma((4,)), dma((9,)), dma((9,)), dma((8,)), dma((8,)), dma((6,)), dma((6,)),
+            dma((2,)), dma((2,)), dma, dma, dma((2,)), dma((2,)),
             pltpu.SemaphoreType.REGULAR((8,)),
         ],
         compiler_params=pltpu.CompilerParams(

time: 55.2 us -> 56.3 us (1.020)
  Pallas kernels: 54.5 us -> 55.5 us
    pallas_call x1, Pallas kernels: 53.7 us -> 54.8 us  [shards(): pl.pallas_call(kernel, out_shape=(jax.ShapeDtypeStruct((2, CX, CY, CZ), f...]
where the time goes in v7:
time: 56.3 us; the launch traced here: 56.2 us
  Pallas kernels  55.5 us (99%)
  between operations  0.64 us (1%)
    pallas_call x1, Pallas kernels, shards(): pl.pallas_call(kernel, out_shape=(jax.ShapeDtypeStruct((2, CX, CY, CZ), f...  54.8 us

profile of v7, /device:TPU:1, one launch (start us, length us, event | category | flops | bytes accessed | tf_op | source)
XLA Modules:
  0.0 56.2 jit_solution(11690314806295168276)
XLA Ops:
  0.6 54.8 %chebyshev_step.1 = (f32[2,16,16,128]{3,2,1,0:T(8,128)S(1)}, f32[2,64]{1,0:T(2,128)S(1)}, f32[2,64]{1,0:T(2,128)S(1)}) custom-call(f32[2,16,16,128]{3,2,1,0:T(8,128)} %bitcast.5, f32[16,16,128]{2,1,0:T(8,128)} %bitcast.6), custom_call_target="tpu_custom_call" | custom-call | tf_op jit(solution)/shard_map/chebyshev_step/pallas_call | solution.py:433
  55.4 0.7 %deliver.1 = (f32[2,16,16,128]{3,2,1,0:T(8,128)}, f32[2,64]{1,0:T(2,128)}, f32[2,64]{1,0:T(2,128)}) custom-call(f32[2,16,16,128]{3,2,1,0:T(8,128)S(1)} %get-tuple-element.9.filtered, f32[2,64]{1,0:T(2,128)S(1)} %get-tuple-element.10.inter, f32[2,64]{1,0:T(2,128)S(1)} %get-tuple-element.11.proj), custom_call_target="tpu_custom_call" | custom-call | tf_op jit(solution)/shard_map/deliver/pallas_call | solution.py:474

commit v8 on v6

--- a/solution.py
+++ b/solution.py
@@ -45,21 +45,13 @@
     return total
 
 
-def part_x(src, j):
-    total = None
-    for s in range(1, reach + 1):
-        term = (-0.5 * second_coeffs[s]) * (src[j + s] + src[j - s])
-        total = term if total is None else total + term
-    return total
-
-
 def far_first(i, half):
     return half + ((i + 1) // 2) * (2 * (i % 2) - 1)
 
 
 def kernel(
     orb_in, pot_in, out_f, out_s, out_p,
-    orb, give, pot, first, fil, zo, zf, zs, acc, hf, gf, gh, g_high, g_low, part, r1, r2, both_cores, tot,
+    orb, give, pot, first, fil, zo, zf, zs, acc, hf, gf, gh, g_high, g_low, part, r1, r2, tot,
     loc_sem, in_send, in_recv, core_send, core_recv, x_send, x_recv,
     a2a_send, a2a_recv, back_send, back_recv, red_send, red_recv, ring,
 ):
@@ -153,7 +145,20 @@
             body(k)
             return 0
 
-        lax.fori_loop(first_layer, first_layer + count, step, 0)
+        lax.fori_loop(first_layer, first_layer + count, step, 0, unroll=2)
+
+    def over_strips(src, first_layer, count, finish):
+        def strip(r, _):
+            at_rows = pl.ds(pl.multiple_of(r * 8, 8), 8)
+            line = [src[first_layer + j, at_rows] for j in range(count + 12)]
+            for i in range(count):
+                total = acc[first_layer + i, at_rows]
+                for s in range(1, reach + 1):
+                    total = total + (-0.5 * second_coeffs[s]) * (line[i + 6 + s] + line[i + 6 - s])
+                finish(first_layer + i, at_rows, line[i + 6], total)
+            return 0
+
+        lax.fori_loop(0, NY // 8, strip, 0, unroll=2)
 
     def along_y(src):
         def body(k):
@@ -181,9 +186,9 @@
         c.start()
         return c
 
-    swaps[2].start()
     beside[0].wait_recv()
     over_layers(along_z_half(rows))
+    swaps[2].start()
     hear(0)
     tell(1)
     swaps[0].wait_recv()
@@ -199,26 +204,25 @@
     over_layers(along_z_half(rows_other))
     given.wait_recv()
 
-    def inner(body):
-        over_layers(body, 6, 4)
-
-    def edges(body, src, k):
-        over_layers(body, 0, 6)
+    def inner(src, finish):
+        over_strips(src, 6, 4, finish)
+
+    def edges(finish, before, src, k):
+        over_strips(before, 0, 6, finish)
         sent = [rim(src, k, False)]
-        over_layers(body, 10, 6)
+        over_strips(before, 10, 6, finish)
         sent.append(rim(src, k + 1, True))
         beside.append(to_mate(k // 2 + 1, src.at[mid], zf if k == 2 else zs))
         return sent
 
-    def last_first(k):
-        here = orb[k + 6]
-        h = acc[k] + hf[k] + part_x(orb, k + 6) + (pot[k] - filter_center) * here
-        first[k + 6] = h * (1.0 / filter_half)
-
-    inner(last_first)
+    def last_first(k, at_rows, here, total):
+        h = total + hf[k, at_rows] + (pot[k, at_rows] - filter_center) * here
+        first[k + 6, at_rows] = h * (1.0 / filter_half)
+
+    inner(orb, last_first)
     for c in direct + rims:
         c.wait_recv()
-    rims += edges(last_first, first, 2)
+    rims += edges(last_first, orb, first, 2)
 
     hear(2)
     tell(3)
@@ -267,16 +271,15 @@
             def _():
                 got[zy] = src[skip + layer_of(k, z), pl.ds(row, 8)]
 
-    def last_filtered(k):
-        here = first[k + 6]
-        h = acc[k] + part_x(first, k + 6) + (pot[k] - filter_center) * here
-        fil[k + 6] = h * (2.0 / filter_half) - orb[k + 6]
-
-    inner(last_filtered)
+    def last_filtered(k, at_rows, here, total):
+        h = total + (pot[k, at_rows] - filter_center) * here
+        fil[k + 6, at_rows] = h * (2.0 / filter_half) - orb[k + 6, at_rows]
+
+    inner(first, last_filtered)
     send_inner(fil, 6, gf, 0)
     for c in rims[2:4]:
         c.wait_recv()
-    rims += edges(last_filtered, fil, 4)
+    rims += edges(last_filtered, first, fil, 4)
 
     def filtered_out(i, _):
         send_tiles(fil, 6, gf, 0, (z + far_first(i, 4)) % 8, (1, 2, 3))
@@ -292,19 +295,19 @@
     hear(5)
     tell(6)
 
-    def applied_layer(k):
-        hf[k] = acc[k] + part_x(fil, k + 6) + pot[k] * fil[k + 6]
+    def last_applied(k, at_rows, here, total):
+        hf[k, at_rows] = total + pot[k, at_rows] * here
 
     beside[3].wait_recv()
     over_layers(along_z(fil, zs))
     hear(6)
     tell(7)
-    inner(applied_layer)
+    inner(fil, last_applied)
     send_inner(hf, 0, gh, 1)
     for c in rims[4:]:
         c.wait_recv()
-    over_layers(applied_layer, 0, 6)
-    over_layers(applied_layer, 10, 6)
+    over_strips(fil, 0, 6, last_applied)
+    over_strips(fil, 10, 6, last_applied)
 
     def applied_out(i, _):
         send_tiles(hf, 0, gh, 1, (z + far_first(i, 4)) % 8, (1, 2, 3))
@@ -332,44 +335,44 @@
         g_high[s] = upper
         g_low[s] = lower
         over = over + (contract(upper, upper) + (contract(upper, lower) + contract(lower, upper)))
-    part[:, :, :NB] = over.reshape(8, 8, NB)
+    part[:, :, :NB] = over.reshape(32, 2, NB)
     all_tiles(gh, 1).wait_recv()
     proj = jnp.zeros((NB, NB), jnp.float32)
     for s in range(4):
         upper, lower = halves(cells(gh, s))
         proj = proj + (contract(g_high[s], upper) + (contract(g_high[s], lower) + contract(g_low[s], upper)))
-    part[:, :, NB:] = proj.reshape(8, 8, NB)
-
-    slot = z * 2 + yl
-
-    sides = [x * 4 + (1 - yl) * 2 + core, domain]
-    for i in range(8):
-        pz = (z + far_first(i, 4)) % 8
-        for to in sides[: 2 if i < 7 else 1]:
-            rdma(part.at[pz], r1.at[slot], red_send.at[0], red_recv.at[0], (pz * 4 + yh, to)).start()
+    part[:, :, NB:] = proj.reshape(32, 2, NB)
+
+    def send_rows(pz, at_home=False):
+        for k in range(8):
+            py = (y + far_first(k, 4)) % 8
+            if not (at_home and k == 7):
+                rdma(
+                    part.at[pz * 4 + py // 2], r1.at[zy], red_send.at[0], red_recv.at[0], at(pz, py, x, core)
+                ).start()
+
+    def rows_out(i, _):
+        send_rows((z + far_first(i, 4)) % 8)
+        return 0
+
+    lax.fori_loop(0, 7, rows_out, 0)
+    send_rows(z, True)
+    r1[zy] = part[band]
+    red1 = rdma(r1.at[pl.ds(0, 63)], r1.at[pl.ds(0, 63)], red_send.at[0], red_recv.at[0], mate)
+    red1.wait_recv()
     back = rdma(fil.at[mid, rows_other], out_f.at[yl], back_send, back_recv, at(z, yo, x, core))
     back.start()
     keep = pltpu.make_async_copy(fil.at[mid, rows], out_f.at[yl], loc_sem.at[2])
     keep.start()
-    r1[slot] = part[z]
-    red1 = rdma(r1.at[pl.ds(0, 15)], r1.at[pl.ds(0, 15)], red_send.at[0], red_recv.at[0], mate)
-    red1.wait_recv()
-
-    both_cores[0] = jnp.sum(r1[...], axis=0)
-    red3 = rdma(both_cores.at[0], both_cores.at[1], red_send.at[2], red_recv.at[2], mate)
-    red3.start()
-    red3.wait_recv()
-    total = both_cores[0] + both_cores[1]
+
+    tot[...] = jnp.sum(r1[...], axis=0)
+    slot = x * 2 + core
     for i in range(4):
-        tot[i] = total[2 * i : 2 * i + 2]
-    slot2 = yh * 4 + x
-    columns = [((x + far_first(i, 2)) % 4) * 4 + yl * 2 + core for i in range(4)]
-    for i in range(4):
-        ph = (yh + far_first(i, 2)) % 4
-        for to in columns[: 4 if i < 3 else 3]:
-            rdma(tot.at[ph], r2.at[slot2], red_send.at[1], red_recv.at[1], (z * 4 + ph, to)).start()
-    r2[slot2] = tot[yh]
-    red2 = rdma(r2.at[pl.ds(0, 15)], r2.at[pl.ds(0, 15)], red_send.at[1], red_recv.at[1], mate)
+        for pc in (1 - core, core)[: 2 if i < 3 else 1]:
+            to = at(z, y, (x + far_first(i, 2)) % 4, pc)
+            rdma(tot, r2.at[slot], red_send.at[1], red_recv.at[1], to).start()
+    r2[slot] = tot[...]
+    red2 = rdma(r2.at[pl.ds(0, 7)], r2.at[pl.ds(0, 7)], red_send.at[1], red_recv.at[1], mate)
     red2.wait_recv()
     result = jnp.sum(r2[...], axis=0) * (1.0 / NCELL)
     out_s[...] = result[:, :NB]
@@ -385,7 +388,6 @@
     all_tiles(gh, 1).wait_send()
     red1.wait_send()
     red2.wait_send()
-    red3.wait_send()
     keep.wait()
     back.wait()
 
@@ -432,13 +434,12 @@
             vmem((NB, 8, CZ), f32),
             vmem((4, NB, 2 * CZ), jnp.bfloat16),
             vmem((4, NB, 2 * CZ), jnp.bfloat16),
-            vmem((8, 8, 2 * NB), f32),
-            vmem((16, 8, 2 * NB), f32),
-            vmem((16, 2, 2 * NB), f32),
-            vmem((2, 8, 2 * NB), f32),
-            vmem((4, 2, 2 * NB), f32),
+            vmem((32, 2, 2 * NB), f32),
+            vmem((64, 2, 2 * NB), f32),
+            vmem((8, 2, 2 * NB), f32),
+            vmem((2, 2 * NB), f32),
             dma((4,)), dma((6,)), dma((6,)), dma((4,)), dma((4,)), dma((6,)), dma((6,)),
-            dma((2,)), dma((2,)), dma, dma, dma((3,)), dma((3,)),
+            dma((2,)), dma((2,)), dma, dma, dma((2,)), dma((2,)),
             pltpu.SemaphoreType.REGULAR((8,)),
         ],
         compiler_params=pltpu.CompilerParams(

time: 55.2 us -> 52.7 us (0.955)
  Pallas kernels: 54.5 us -> 52 us
    pallas_call x1, Pallas kernels: 53.7 us -> 51.2 us  [shards(): pl.pallas_call(kernel, out_shape=(jax.ShapeDtypeStruct((2, CX, CY, CZ), f...]
where the time goes in v8:
time: 52.7 us; the launch traced here: 52.6 us
  Pallas kernels  52 us (99%)
  between operations  0.64 us (1%)
    pallas_call x1, Pallas kernels, shards(): pl.pallas_call(kernel, out_shape=(jax.ShapeDtypeStruct((2, CX, CY, CZ), f...  51.2 us

profile of v8, /device:TPU:1, one launch (start us, length us, event | category | flops | bytes accessed | tf_op | source)
XLA Modules:
  0.0 52.6 jit_solution(15141773792059398662)
XLA Ops:
  0.6 51.2 %chebyshev_step.1 = (f32[2,16,16,128]{3,2,1,0:T(8,128)S(1)}, f32[2,64]{1,0:T(2,128)S(1)}, f32[2,64]{1,0:T(2,128)S(1)}) custom-call(f32[2,16,16,128]{3,2,1,0:T(8,128)} %bitcast.5, f32[16,16,128]{2,1,0:T(8,128)} %bitcast.6), custom_call_target="tpu_custom_call" | custom-call | tf_op jit(solution)/shard_map/chebyshev_step/pallas_call | solution.py:413
  51.9 0.7 %deliver.1 = (f32[2,16,16,128]{3,2,1,0:T(8,128)}, f32[2,64]{1,0:T(2,128)}, f32[2,64]{1,0:T(2,128)}) custom-call(f32[2,16,16,128]{3,2,1,0:T(8,128)S(1)} %get-tuple-element.9.filtered, f32[2,64]{1,0:T(2,128)S(1)} %get-tuple-element.10.inter, f32[2,64]{1,0:T(2,128)S(1)} %get-tuple-element.11.proj), custom_call_target="tpu_custom_call" | custom-call | tf_op jit(solution)/shard_map/deliver/pallas_call | solution.py:453

commit v9 on v8

--- a/solution.py
+++ b/solution.py
@@ -147,9 +147,9 @@
 
         lax.fori_loop(first_layer, first_layer + count, step, 0, unroll=2)
 
-    def over_strips(src, first_layer, count, finish):
+    def over_strips(src, first_layer, count, finish, base=0, strips=NY // 8):
         def strip(r, _):
-            at_rows = pl.ds(pl.multiple_of(r * 8, 8), 8)
+            at_rows = pl.ds(pl.multiple_of(base + r * 8, 8), 8)
             line = [src[first_layer + j, at_rows] for j in range(count + 12)]
             for i in range(count):
                 total = acc[first_layer + i, at_rows]
@@ -158,7 +158,7 @@
                 finish(first_layer + i, at_rows, line[i + 6], total)
             return 0
 
-        lax.fori_loop(0, NY // 8, strip, 0, unroll=2)
+        lax.fori_loop(0, strips, strip, 0, unroll=2)
 
     def along_y(src):
         def body(k):
@@ -207,12 +207,16 @@
     def inner(src, finish):
         over_strips(src, 6, 4, finish)
 
-    def edges(finish, before, src, k):
-        over_strips(before, 0, 6, finish)
-        sent = [rim(src, k, False)]
-        over_strips(before, 10, 6, finish)
-        sent.append(rim(src, k + 1, True))
-        beside.append(to_mate(k // 2 + 1, src.at[mid], zf if k == 2 else zs))
+    def edges(finish, before, arriving, src, k):
+        sent = []
+        for h, (base, at_rows) in enumerate(((mine, rows), (other, rows_other))):
+            for c in arriving[h]:
+                c.wait_recv()
+            over_strips(before, 0, 6, finish, base, 2)
+            sent.append([rim(src, k + 2 * h, False, at_rows)])
+            over_strips(before, 10, 6, finish, base, 2)
+            sent[h].append(rim(src, k + 2 * h + 1, True, at_rows))
+        beside.append(to_mate(k // 4 + 2, src.at[mid], zf if k == 2 else zs))
         return sent
 
     def last_first(k, at_rows, here, total):
@@ -220,9 +224,7 @@
         first[k + 6, at_rows] = h * (1.0 / filter_half)
 
     inner(orb, last_first)
-    for c in direct + rims:
-        c.wait_recv()
-    rims += edges(last_first, orb, first, 2)
+    rims_first = edges(last_first, orb, (direct, rims), first, 2)
 
     hear(2)
     tell(3)
@@ -238,9 +240,9 @@
         m = pz // 2
         return (6 + m, m, 4 + m + 4 * (m // 2), 12 + m)[group]
 
-    def send_tiles(src, skip, got, which, pz, groups, at_home=False):
+    def send_tiles(src, skip, got, which, pz, groups, at_home=False, parts=(0, 1)):
         for group in groups:
-            for b in range(2):
+            for b in parts:
                 py = (pz + group + 4 * b) % 8
                 row = pl.multiple_of(16 * b + 8 * (pz % 2), 8)
                 copy = rdma(
@@ -255,13 +257,19 @@
     def all_tiles(got, which):
         return rdma(got.at[pl.ds(0, 63)], got.at[pl.ds(0, 63)], a2a_send.at[which], a2a_recv.at[which], mate)
 
-    def send_inner(src, skip, got, which):
+    def send_all(src, skip, got, which, groups, parts=(0, 1), work=None):
         def turn(i, _):
-            send_tiles(src, skip, got, which, (z + far_first(i, 4)) % 8, (0,))
+            send_tiles(src, skip, got, which, (z + far_first(i, 4)) % 8, groups, False, parts)
+            if work is not None:
+                work(2 * i)
+                work(2 * i + 1)
             return 0
 
         lax.fori_loop(0, 7, turn, 0)
-        send_tiles(src, skip, got, which, z, (0,), True)
+        send_tiles(src, skip, got, which, z, groups, True, parts)
+        if work is not None:
+            work(14)
+            work(15)
 
     def keep_tile(src, skip, got):
         group, b = (y + 8 - z) % 4, ((y + 8 - z) % 8) // 4
@@ -276,22 +284,10 @@
         fil[k + 6, at_rows] = h * (2.0 / filter_half) - orb[k + 6, at_rows]
 
     inner(first, last_filtered)
-    send_inner(fil, 6, gf, 0)
-    for c in rims[2:4]:
-        c.wait_recv()
-    rims += edges(last_filtered, first, fil, 4)
-
-    def filtered_out(i, _):
-        send_tiles(fil, 6, gf, 0, (z + far_first(i, 4)) % 8, (1, 2, 3))
-        for j in (2 * i, 2 * i + 1):
-            acc[j] = part_y(fil[j + 6])
-        return 0
-
-    lax.fori_loop(0, 7, filtered_out, 0)
-    send_tiles(fil, 6, gf, 0, z, (1, 2, 3), True)
+    rims_filtered = edges(last_filtered, first, rims_first, fil, 6)
+
+    send_all(fil, 6, gf, 0, (0, 1), work=along_y(fil))
     keep_tile(fil, 6, gf)
-    for j in (14, 15):
-        acc[j] = part_y(fil[j + 6])
     hear(5)
     tell(6)
 
@@ -299,22 +295,17 @@
         hf[k, at_rows] = total + pot[k, at_rows] * here
 
     beside[3].wait_recv()
-    over_layers(along_z(fil, zs))
+    send_all(fil, 6, gf, 0, (2, 3), work=along_z(fil, zs))
     hear(6)
     tell(7)
     inner(fil, last_applied)
-    send_inner(hf, 0, gh, 1)
-    for c in rims[4:]:
-        c.wait_recv()
-    over_strips(fil, 0, 6, last_applied)
-    over_strips(fil, 10, 6, last_applied)
-
-    def applied_out(i, _):
-        send_tiles(hf, 0, gh, 1, (z + far_first(i, 4)) % 8, (1, 2, 3))
-        return 0
-
-    lax.fori_loop(0, 7, applied_out, 0)
-    send_tiles(hf, 0, gh, 1, z, (1, 2, 3), True)
+    send_all(hf, 0, gh, 1, (0,))
+    for h, base in enumerate((mine, other)):
+        for c in rims_filtered[h]:
+            c.wait_recv()
+        over_strips(fil, 0, 6, last_applied, base, 2)
+        over_strips(fil, 10, 6, last_applied, base, 2)
+        send_all(hf, 0, gh, 1, (1, 2, 3), (yl if h == 0 else 1 - yl,))
     keep_tile(hf, 0, gh)
 
     def contract(left, right):
@@ -357,14 +348,13 @@
 
     lax.fori_loop(0, 7, rows_out, 0)
     send_rows(z, True)
-    r1[zy] = part[band]
-    red1 = rdma(r1.at[pl.ds(0, 63)], r1.at[pl.ds(0, 63)], red_send.at[0], red_recv.at[0], mate)
-    red1.wait_recv()
     back = rdma(fil.at[mid, rows_other], out_f.at[yl], back_send, back_recv, at(z, yo, x, core))
     back.start()
     keep = pltpu.make_async_copy(fil.at[mid, rows], out_f.at[yl], loc_sem.at[2])
     keep.start()
-
+    r1[zy] = part[band]
+    red1 = rdma(r1.at[pl.ds(0, 63)], r1.at[pl.ds(0, 63)], red_send.at[0], red_recv.at[0], mate)
+    red1.wait_recv()
     tot[...] = jnp.sum(r1[...], axis=0)
     slot = x * 2 + core
     for i in range(4):
@@ -378,11 +368,13 @@
     out_s[...] = result[:, :NB]
     out_p[...] = result[:, NB:]
 
-    for c in swaps + direct + [given]:
+    for c in swaps + direct + [given] + rims:
         c.wait_send()
     for c in beside:
         c.wait_send()
-    for c in rims:
+    for c in sum(rims_first, []):
+        c.wait_send()
+    for c in sum(rims_filtered, []):
         c.wait_send()
     all_tiles(gf, 0).wait_send()
     all_tiles(gh, 1).wait_send()
@@ -438,7 +430,7 @@
             vmem((64, 2, 2 * NB), f32),
             vmem((8, 2, 2 * NB), f32),
             vmem((2, 2 * NB), f32),
-            dma((4,)), dma((6,)), dma((6,)), dma((4,)), dma((4,)), dma((6,)), dma((6,)),
+            dma((4,)), dma((6,)), dma((6,)), dma((4,)), dma((4,)), dma((10,)), dma((10,)),
             dma((2,)), dma((2,)), dma, dma, dma((2,)), dma((2,)),
             pltpu.SemaphoreType.REGULAR((8,)),
         ],

time: 52.7 us -> 53.9 us (1.023)
  Pallas kernels: 52 us -> 53.1 us
    pallas_call x1, Pallas kernels: 51.2 us -> 52.4 us  [shards(): pl.pallas_call(kernel, out_shape=(jax.ShapeDtypeStruct((2, CX, CY, CZ), f...]
where the time goes in v9:
time: 53.9 us; the launch traced here: 53.8 us
  Pallas kernels  53.1 us (99%)
  between operations  0.64 us (1%)
    pallas_call x1, Pallas kernels, shards(): pl.pallas_call(kernel, out_shape=(jax.ShapeDtypeStruct((2, CX, CY, CZ), f...  52.4 us

profile of v9, /device:TPU:1, one launch (start us, length us, event | category | flops | bytes accessed | tf_op | source)
XLA Modules:
  0.0 53.8 jit_solution(10954358507129156773)
XLA Ops:
  0.6 52.4 %chebyshev_step.1 = (f32[2,16,16,128]{3,2,1,0:T(8,128)S(1)}, f32[2,64]{1,0:T(2,128)S(1)}, f32[2,64]{1,0:T(2,128)S(1)}) custom-call(f32[2,16,16,128]{3,2,1,0:T(8,128)} %bitcast.5, f32[16,16,128]{2,1,0:T(8,128)} %bitcast.6), custom_call_target="tpu_custom_call" | custom-call | tf_op jit(solution)/shard_map/chebyshev_step/pallas_call | solution.py:405
  53.0 0.7 %deliver.1 = (f32[2,16,16,128]{3,2,1,0:T(8,128)}, f32[2,64]{1,0:T(2,128)}, f32[2,64]{1,0:T(2,128)}) custom-call(f32[2,16,16,128]{3,2,1,0:T(8,128)S(1)} %get-tuple-element.9.filtered, f32[2,64]{1,0:T(2,128)S(1)} %get-tuple-element.10.inter, f32[2,64]{1,0:T(2,128)S(1)} %get-tuple-element.11.proj), custom_call_target="tpu_custom_call" | custom-call | tf_op jit(solution)/shard_map/deliver/pallas_call | solution.py:445

commit v10 on v9

--- a/solution.py
+++ b/solution.py
@@ -46,7 +46,7 @@
 
 
 def far_first(i, half):
-    return half + ((i + 1) // 2) * (2 * (i % 2) - 1)
+    return half + ((i + 1) >> 1) * (2 * (i & 1) - 1)
 
 
 def kernel(
@@ -57,19 +57,19 @@
 ):
     band = lax.axis_index("band")
     domain = lax.axis_index("domain")
-    z, yh = band // 4, band % 4
-    x, yl, core = domain // 4, (domain // 2) % 2, domain % 2
+    z, yh = band >> 2, band & 3
+    x, yl, core = domain >> 2, (domain >> 1) & 1, domain & 1
     y = yh * 2 + yl
     zy = z * 8 + y
     mine = pl.multiple_of(yl * CY, CY)
     other = pl.multiple_of((1 - yl) * CY, CY)
 
     def at(pz, py, px, pc):
-        return (pz * 4 + py // 2, px * 4 + (py % 2) * 2 + pc)
-
-    xn, xp = (x + 1) % 4, (x + 3) % 4
+        return ((pz << 2) + (py >> 1), (px << 2) + ((py & 1) << 1) + pc)
+
+    xn, xp = (x + 1) & 3, (x + 3) & 3
     yo = y + 1 - 2 * yl
-    yq = (y + 7 + 2 * yl) % 8
+    yq = (y + 7 + 2 * yl) & 7
     mate = at(z, y, x, 1 - core)
     to_xn, to_xp = at(z, y, xn, core), at(z, y, xp, core)
 
@@ -93,16 +93,16 @@
         c.start()
 
     bar = pltpu.get_barrier_semaphore()
-    up_z, down_z = at((z + 1) % 8, y, x, core), at((z + 7) % 8, y, x, core)
-    up_y, down_y = at(z, (y + 1) % 8, x, core), at(z, (y + 7) % 8, x, core)
+    up_z, down_z = at((z + 1) & 7, y, x, core), at((z + 7) & 7, y, x, core)
+    up_y, down_y = at(z, (y + 1) & 7, x, core), at(z, (y + 7) & 7, x, core)
     for to in (up_y, down_y, to_xn, to_xp, up_z, down_z, mate):
         pl.semaphore_signal(bar, inc=1, device_id=to, device_id_type=MESH)
     pl.semaphore_wait(bar, 7)
     for c in local:
         c.wait()
 
-    far_z = (at((z + 2) % 8, y, x, core), at((z + 6) % 8, y, x, core))
-    far_y = (at(z, (y + 2) % 8, x, core), at(z, (y + 6) % 8, x, core))
+    far_z = (at((z + 2) & 7, y, x, core), at((z + 6) & 7, y, x, core))
+    far_y = (at(z, (y + 2) & 7, x, core), at(z, (y + 6) & 7, x, core))
     words = (
         (up_z, down_z), far_z, (up_y, down_y), (up_y, down_y), far_y, (mate,), (to_xn, to_xp), (to_xn, to_xp),
     )
@@ -237,14 +237,14 @@
     tell(5)
 
     def layer_of(group, pz):
-        m = pz // 2
-        return (6 + m, m, 4 + m + 4 * (m // 2), 12 + m)[group]
+        m = pz >> 1
+        return (6 + m, m, 4 + m + ((m >> 1) << 2), 12 + m)[group]
 
     def send_tiles(src, skip, got, which, pz, groups, at_home=False, parts=(0, 1)):
         for group in groups:
             for b in parts:
-                py = (pz + group + 4 * b) % 8
-                row = pl.multiple_of(16 * b + 8 * (pz % 2), 8)
+                py = (pz + group + 4 * b) & 7
+                row = pl.multiple_of(16 * b + ((pz & 1) << 3), 8)
                 copy = rdma(
                     src.at[skip + layer_of(group, pz), pl.ds(row, 8)], got.at[zy],
                     a2a_send.at[which], a2a_recv.at[which], at(pz, py, x, core),
@@ -259,7 +259,7 @@
 
     def send_all(src, skip, got, which, groups, parts=(0, 1), work=None):
         def turn(i, _):
-            send_tiles(src, skip, got, which, (z + far_first(i, 4)) % 8, groups, False, parts)
+            send_tiles(src, skip, got, which, (z + far_first(i, 4)) & 7, groups, False, parts)
             if work is not None:
                 work(2 * i)
                 work(2 * i + 1)
@@ -272,8 +272,8 @@
             work(15)
 
     def keep_tile(src, skip, got):
-        group, b = (y + 8 - z) % 4, ((y + 8 - z) % 8) // 4
-        row = pl.multiple_of(16 * b + 8 * (z % 2), 8)
+        group, b = (y + 8 - z) & 3, ((y + 8 - z) & 7) >> 2
+        row = pl.multiple_of(16 * b + ((z & 1) << 3), 8)
         for k in range(4):
             @pl.when(group == k)
             def _():
@@ -284,9 +284,10 @@
         fil[k + 6, at_rows] = h * (2.0 / filter_half) - orb[k + 6, at_rows]
 
     inner(first, last_filtered)
+    send_all(fil, 6, gf, 0, (0,))
     rims_filtered = edges(last_filtered, first, rims_first, fil, 6)
 
-    send_all(fil, 6, gf, 0, (0, 1), work=along_y(fil))
+    send_all(fil, 6, gf, 0, (1, 2, 3), work=along_y(fil))
     keep_tile(fil, 6, gf)
     hear(5)
     tell(6)
@@ -295,7 +296,7 @@
         hf[k, at_rows] = total + pot[k, at_rows] * here
 
     beside[3].wait_recv()
-    send_all(fil, 6, gf, 0, (2, 3), work=along_z(fil, zs))
+    over_layers(along_z(fil, zs))
     hear(6)
     tell(7)
     inner(fil, last_applied)
@@ -305,7 +306,7 @@
             c.wait_recv()
         over_strips(fil, 0, 6, last_applied, base, 2)
         over_strips(fil, 10, 6, last_applied, base, 2)
-        send_all(hf, 0, gh, 1, (1, 2, 3), (yl if h == 0 else 1 - yl,))
+    send_all(hf, 0, gh, 1, (1, 2, 3))
     keep_tile(hf, 0, gh)
 
     def contract(left, right):
@@ -336,14 +337,14 @@
 
     def send_rows(pz, at_home=False):
         for k in range(8):
-            py = (y + far_first(k, 4)) % 8
+            py = (y + far_first(k, 4)) & 7
             if not (at_home and k == 7):
                 rdma(
-                    part.at[pz * 4 + py // 2], r1.at[zy], red_send.at[0], red_recv.at[0], at(pz, py, x, core)
+                    part.at[(pz << 2) + (py >> 1)], r1.at[zy], red_send.at[0], red_recv.at[0], at(pz, py, x, core)
                 ).start()
 
     def rows_out(i, _):
-        send_rows((z + far_first(i, 4)) % 8)
+        send_rows((z + far_first(i, 4)) & 7)
         return 0
 
     lax.fori_loop(0, 7, rows_out, 0)
@@ -359,7 +360,7 @@
     slot = x * 2 + core
     for i in range(4):
         for pc in (1 - core, core)[: 2 if i < 3 else 1]:
-            to = at(z, y, (x + far_first(i, 2)) % 4, pc)
+            to = at(z, y, (x + far_first(i, 2)) & 3, pc)
             rdma(tot, r2.at[slot], red_send.at[1], red_recv.at[1], to).start()
     r2[slot] = tot[...]
     red2 = rdma(r2.at[pl.ds(0, 7)], r2.at[pl.ds(0, 7)], red_send.at[1], red_recv.at[1], mate)

time: 53.9 us -> 52.4 us (0.972)
  Pallas kernels: 53.1 us -> 51.7 us
    pallas_call x1, Pallas kernels: 52.4 us -> 50.9 us  [shards(): pl.pallas_call(kernel, out_shape=(jax.ShapeDtypeStruct((2, CX, CY, CZ), f...]
where the time goes in v10:
time: 52.4 us; the launch traced here: 52.3 us
  Pallas kernels  51.7 us (99%)
  between operations  0.64 us (1%)
    pallas_call x1, Pallas kernels, shards(): pl.pallas_call(kernel, out_shape=(jax.ShapeDtypeStruct((2, CX, CY, CZ), f...  50.9 us

profile of v10, /device:TPU:1, one launch (start us, length us, event | category | flops | bytes accessed | tf_op | source)
XLA Modules:
  0.0 52.3 jit_solution(10145493815202034070)
XLA Ops:
  0.6 50.9 %chebyshev_step.1 = (f32[2,16,16,128]{3,2,1,0:T(8,128)S(1)}, f32[2,64]{1,0:T(2,128)S(1)}, f32[2,64]{1,0:T(2,128)S(1)}) custom-call(f32[2,16,16,128]{3,2,1,0:T(8,128)} %bitcast.5, f32[16,16,128]{2,1,0:T(8,128)} %bitcast.6), custom_call_target="tpu_custom_call" | custom-call | tf_op jit(solution)/shard_map/chebyshev_step/pallas_call | solution.py:406
  51.6 0.7 %deliver.1 = (f32[2,16,16,128]{3,2,1,0:T(8,128)}, f32[2,64]{1,0:T(2,128)}, f32[2,64]{1,0:T(2,128)}) custom-call(f32[2,16,16,128]{3,2,1,0:T(8,128)S(1)} %get-tuple-element.9.filtered, f32[2,64]{1,0:T(2,128)S(1)} %get-tuple-element.10.inter, f32[2,64]{1,0:T(2,128)S(1)} %get-tuple-element.11.proj), custom_call_target="tpu_custom_call" | custom-call | tf_op jit(solution)/shard_map/deliver/pallas_call | solution.py:446

commit v11 on v10

--- a/solution.py
+++ b/solution.py
@@ -349,13 +349,21 @@
 
     lax.fori_loop(0, 7, rows_out, 0)
     send_rows(z, True)
-    back = rdma(fil.at[mid, rows_other], out_f.at[yl], back_send, back_recv, at(z, yo, x, core))
-    back.start()
+    def give_back(k):
+        c = rdma(
+            fil.at[pl.ds(6 + 8 * k, 8), rows_other], out_f.at[yl, pl.ds(8 * k, 8)],
+            back_send.at[k], back_recv.at[k], at(z, yo, x, core),
+        )
+        c.start()
+        return c
+
+    back = [give_back(0)]
     keep = pltpu.make_async_copy(fil.at[mid, rows], out_f.at[yl], loc_sem.at[2])
     keep.start()
     r1[zy] = part[band]
     red1 = rdma(r1.at[pl.ds(0, 63)], r1.at[pl.ds(0, 63)], red_send.at[0], red_recv.at[0], mate)
     red1.wait_recv()
+    back.append(give_back(1))
     tot[...] = jnp.sum(r1[...], axis=0)
     slot = x * 2 + core
     for i in range(4):
@@ -382,7 +390,8 @@
     red1.wait_send()
     red2.wait_send()
     keep.wait()
-    back.wait()
+    for c in back:
+        c.wait()
 
 
 def deliver(filtered, inter, proj, out_f, out_s, out_p, sem):
@@ -432,7 +441,7 @@
             vmem((8, 2, 2 * NB), f32),
             vmem((2, 2 * NB), f32),
             dma((4,)), dma((6,)), dma((6,)), dma((4,)), dma((4,)), dma((10,)), dma((10,)),
-            dma((2,)), dma((2,)), dma, dma, dma((2,)), dma((2,)),
+            dma((2,)), dma((2,)), dma((2,)), dma((2,)), dma((2,)), dma((2,)),
             pltpu.SemaphoreType.REGULAR((8,)),
         ],
         compiler_params=pltpu.CompilerParams(

time: 52.4 us -> 52.4 us (level)
  no operation moved by 1% of the time
where the time goes in v11:
time: 52.4 us; the launch traced here: 52.3 us
  Pallas kernels  51.7 us (99%)
  between operations  0.64 us (1%)
    pallas_call x1, Pallas kernels, shards(): pl.pallas_call(kernel, out_shape=(jax.ShapeDtypeStruct((2, CX, CY, CZ), f...  50.9 us

profile of v11, /device:TPU:1, one launch (start us, length us, event | category | flops | bytes accessed | tf_op | source)
XLA Modules:
  0.0 52.3 jit_solution(11768360504782747466)
XLA Ops:
  0.6 50.9 %chebyshev_step.1 = (f32[2,16,16,128]{3,2,1,0:T(8,128)S(1)}, f32[2,64]{1,0:T(2,128)S(1)}, f32[2,64]{1,0:T(2,128)S(1)}) custom-call(f32[2,16,16,128]{3,2,1,0:T(8,128)} %bitcast.5, f32[16,16,128]{2,1,0:T(8,128)} %bitcast.6), custom_call_target="tpu_custom_call" | custom-call | tf_op jit(solution)/shard_map/chebyshev_step/pallas_call | solution.py:415
  51.6 0.7 %deliver.1 = (f32[2,16,16,128]{3,2,1,0:T(8,128)}, f32[2,64]{1,0:T(2,128)}, f32[2,64]{1,0:T(2,128)}) custom-call(f32[2,16,16,128]{3,2,1,0:T(8,128)S(1)} %get-tuple-element.9.filtered, f32[2,64]{1,0:T(2,128)S(1)} %get-tuple-element.10.inter, f32[2,64]{1,0:T(2,128)S(1)} %get-tuple-element.11.proj), custom_call_target="tpu_custom_call" | custom-call | tf_op jit(solution)/shard_map/deliver/pallas_call | solution.py:455
